TPU v7x, 256 devices: a whole 4x4x8 slice. The times are simulated.
256 devices in a mesh: pts: 16 (over z_hi, x, core), cen: 16 (over y, z_lo).
Axes of the slice: x: 4, y: 4, z: 8 (z_hi: 2, z_lo: 4; z = z_hi * 4 + z_lo), core: 2. Of those that a mesh axis runs over, the one named last changes fastest.
Arguments:
- sample_vectors: float32 [12288, 1024], P('pts'), may hold values from -4 to 4
- centroids: float32 [1024, 16384], P(None, 'cen'), may hold values from -1 to 1
Outputs:
- responsibilities: float32 [12288, 16384], P('pts', 'cen')
- new_centroids: float32 [1024, 16384], P('pts', 'cen')
All inputs are finite; a program needn't handle non-finite values.
Results may differ from a plain program's by a relative error of at most 0.00075.
Values sent between devices are 32-bit elements; how exact they have to be, the bound alone decides.
No kernel may reach another device: no remote copies, remote signals or barrier semaphores. Data moves between devices by JAX's collectives and lax.ppermute only.
A program may use at most 128 MiB of HBM per device.

v0:
```python
import jax
import jax.numpy as jnp
from jax import lax
from jax.sharding import PartitionSpec as P

smoothing_divisor = 0.1
prior_weight = 1.0


def soft_weights(raw_affinity, prototype_sq_length):
    membership_affinity = (raw_affinity - 0.5 * prototype_sq_length) / smoothing_divisor
    local_top = jnp.max(membership_affinity, axis=1, keepdims=True)
    top = lax.pmax(local_top, "cen")
    expo = jnp.exp(membership_affinity - top)
    total = lax.psum(jnp.sum(expo, axis=1, keepdims=True), "cen")
    return expo / total


def count_sum(weights):
    return lax.psum(jnp.sum(weights, axis=0), "pts")


def moment_share(sample_vectors, weights, old_rows, cluster_mass):
    share = lax.psum_scatter(
        lax.dot_general(
            sample_vectors,
            weights,
            (((0,), (0,)), ((), ())),
            precision=lax.Precision.HIGHEST,
            preferred_element_type=jnp.float32,
        ),
        "pts",
        scatter_dimension=0,
        tiled=True,
    )
    return (share + prior_weight * old_rows) / (cluster_mass + prior_weight)


def own_rows(matrix, rows):
    return lax.dynamic_slice_in_dim(matrix, lax.axis_index("pts") * rows, rows, 0)


def local(sample_vectors, centroids):
    high = lax.Precision.HIGHEST
    rows = sample_vectors.shape[1] // lax.axis_size("pts")
    raw_affinity = jnp.dot(
        sample_vectors, centroids, precision=high, preferred_element_type=jnp.float32
    )
    weights = soft_weights(raw_affinity, jnp.sum(centroids * centroids, axis=0))
    cluster_mass = count_sum(weights)
    share = moment_share(sample_vectors, weights, own_rows(centroids, rows), cluster_mass)
    piece = lax.all_gather(share, "pts", axis=0, tiled=True)
    raw_affinity = jnp.dot(
        sample_vectors, piece, precision=high, preferred_element_type=jnp.float32
    )
    prototype_sq_length = jnp.sum(piece * piece, axis=0)
    weights = soft_weights(raw_affinity, prototype_sq_length)
    cluster_mass = count_sum(weights)
    final_rows = moment_share(sample_vectors, weights, share, cluster_mass)
    return (weights, final_rows)


def solution(mesh):
    placed = (P("pts", None), P(None, "cen"))
    return jax.shard_map(
        local,
        mesh=mesh,
        in_specs=placed,
        out_specs=(P("pts", "cen"), P("pts", "cen")),
        check_vma=False,
    )
```

profile of v0, /device:TPU:8, one launch (start us, length us, event | category | flops | bytes accessed | tf_op | source)
XLA Modules:
  0.0 548.0 jit_solution(10219965989971744510)
XLA Ops:
  7.2 0.0 copy-start
  7.2 0.0 reduce-scatter.7.cloned.1.call-start
  7.2 0.0 copy-start.1
  7.2 2.7 multiply_reduce_fusion.1
  9.9 0.4 copy-done
  10.3 1.3 copy-done.1
  11.6 11.8 %fusion = (f32[768]{0:T(1024)S(1)}, f32[768,1024]{1,0:T(8,128)}) fusion(f32[1024]{0:T(1024)S(1)} %broadcast_multiply_fusion.1, f32[768,1024]{1,0:T(8,128)S(1)} %copy-done, f32[1024,1024]{1,0:T(8,128)S(1)} %copy-done.1), kind=kOutput, calls=%fused_computation.6 | convolution fusion | flops 9666034688 | bytes 10492928 | tf_op jit(solution)/shard_map/dot_general | solution.py:46
  23.4 37.9 %pmax.14 = f32[768]{0:T(1024)S(1)} all-reduce(f32[768]{0:T(1024)S(1)} %get-tuple-element.8), channel_id=1, replica_groups=mesh['pts'=16,'cen'=16] {'cen'}, use_global_device_ids=true, to_apply=%region_2.0 | all-reduce | flops 768 | bytes 6144 | tf_op jit(solution)/shard_map/pmax | solution.py:13
  61.3 2.6 fusion.3
  64.0 38.5 %psum.28 = f32[768]{0:T(1024)S(1)} all-reduce(f32[768]{0:T(1024)S(1)} %fusion.3), channel_id=1, replica_groups=mesh['pts'=16,'cen'=16] {'cen'}, use_global_device_ids=true, to_apply=%region_4.0 | all-reduce | flops 768 | bytes 6144 | tf_op jit(solution)/shard_map/psum | solution.py:15
  102.5 13.5 %convolution_bitcast_fusion.1 = f32[1024,1024]{0,1:T(8,128)} fusion(f32[768,1024]{1,0:T(8,128)S(1)} %copy-done, f32[768,1024]{1,0:T(8,128)} %get-tuple-element.9, f32[768]{0:T(1024)S(1)} %psum.28, f32[768]{0:T(1024)S(1)} %pmax.14, f32[1024]{0:T(1024)S(1)} %broadcast_multiply_fusion.1), kind=kOutput, calls=%fused_computation.13 | convolution fusion | flops 9666822144 | bytes 10496000 | tf_op jit(solution)/shard_map/dot_general | solution.py:25
  116.0 5.3 copy.11
  121.3 0.0 reduce-scatter.7.cloned.1.call-update
  121.4 0.0 all-gather.2.cloned.1.call-start
  121.4 1.0 constant_dynamic-slice_fusion
  122.4 1.1 copy.15
  123.4 2.7 fusion.6
  126.1 42.8 %psum.29 = f32[1024]{0:T(1024)S(1)} all-reduce(f32[1024]{0:T(1024)S(1)} %fusion.6), channel_id=1, replica_groups=mesh['pts'=16,'cen'=16] {'pts'}, use_global_device_ids=true, to_apply=%region_7.0 | all-reduce | flops 1024 | bytes 8192 | tf_op jit(solution)/shard_map/psum | solution.py:20
  168.9 62.1 %reduce-scatter.7.cloned.1.call-done = f32[64,1024]{1,0:T(8,128)} async-done(((f32[1024,1024]{1,0:T(8,128)}), f32[64,1024]{1,0:T(8,128)}) %reduce-scatter.7.cloned.1.call-update) | async-done | bytes 262160
  231.0 1.9 copy.12
  233.0 2.3 add_divide_fusion.1
  235.2 1.9 copy.8
  237.1 0.0 all-gather.2.cloned.1.call-update
  237.2 0.2 reduce-scatter.9.cloned.1.call-start
  237.4 72.7 %all-gather.2.cloned.1.call-done = f32[1024,1024]{1,0:T(8,128)} async-done(((f32[64,1024]{1,0:T(8,128)}), f32[1024,1024]{1,0:T(8,128)}) %all-gather.2.cloned.1.call-update) | async-done | bytes 4194320 | tf_op jit(solution)/shard_map/all_gather | solution.py:52
  310.1 0.0 copy-start.2
  310.1 2.7 multiply_reduce_fusion
  312.8 0.8 copy-done.2
  313.6 21.7 %fusion.1 = (f32[768]{0:T(1024)S(1)}, f32[1024,768]{1,0:T(8,128)}) fusion(f32[1024]{0:T(1024)S(1)} %broadcast_multiply_fusion, f32[1024,1024]{1,0:T(8,128)S(1)} %copy-done.2, f32[768,1024]{1,0:T(8,128)S(1)} %copy-done), kind=kOutput, calls=%fused_computation.7 | convolution fusion | flops 9666034688 | bytes 10492928 | tf_op jit(solution)/shard_map/dot_general | solution.py:53
  335.2 33.7 %pmax.15 = f32[768]{0:T(1024)S(1)} all-reduce(f32[768]{0:T(1024)S(1)} %get-tuple-element.10), channel_id=1, replica_groups=mesh['pts'=16,'cen'=16] {'cen'}, use_global_device_ids=true, to_apply=%region_10.0 | all-reduce | flops 768 | bytes 6144 | tf_op jit(solution)/shard_map/pmax | solution.py:13
  368.9 2.6 fusion.4
  371.5 38.2 %psum.30 = f32[768]{0:T(1024)S(1)} all-reduce(f32[768]{0:T(1024)S(1)} %fusion.4), channel_id=1, replica_groups=mesh['pts'=16,'cen'=16] {'cen'}, use_global_device_ids=true, to_apply=%region_12.0 | all-reduce | flops 768 | bytes 6144 | tf_op jit(solution)/shard_map/psum | solution.py:15
  409.7 13.7 %convolution_bitcast_fusion = f32[1024,1024]{0,1:T(8,128)} fusion(f32[768,1024]{1,0:T(8,128)S(1)} %copy-done, f32[1024,768]{1,0:T(8,128)} %get-tuple-element.11, f32[768]{0:T(1024)S(1)} %psum.30, f32[768]{0:T(1024)S(1)} %pmax.15, f32[1024]{0:T(1024)S(1)} %broadcast_multiply_fusion), kind=kOutput, calls=%fused_computation.12 | convolution fusion | flops 9666822144 | bytes 10496000 | tf_op jit(solution)/shard_map/dot_general | solution.py:25
  423.4 5.3 copy.13
  428.8 0.0 reduce-scatter.9.cloned.1.call-update
  428.8 4.4 fusion.9
  433.2 3.5 copy.9
  436.8 42.8 %psum.31 = f32[1024]{0:T(1024)S(1)} all-reduce(f32[1024]{0:T(1024)S(1)} %get-tuple-element.6), channel_id=1, replica_groups=mesh['pts'=16,'cen'=16] {'pts'}, use_global_device_ids=true, to_apply=%region_15.0 | all-reduce | flops 1024 | bytes 8192 | tf_op jit(solution)/shard_map/psum | solution.py:20
  479.5 55.4 %reduce-scatter.9.cloned.1.call-done = f32[64,1024]{1,0:T(8,128)} async-done(((f32[1024,1024]{1,0:T(8,128)}), f32[64,1024]{1,0:T(8,128)}) %reduce-scatter.9.cloned.1.call-update) | async-done | bytes 262160
  535.0 1.9 copy.14
  536.9 2.2 add_divide_fusion
  539.1 1.9 copy.10
  (4 shorter events, 0.0 us)
Async XLA Ops:
  7.2 3.2 copy-start
  7.2 223.8 %reduce-scatter.7.cloned.1.call-start = ((), (), s32[]{:S(2)}) async-start(), calls=%async_computation.3 | async-start | bytes 4456448
  7.2 4.4 copy-start.1
  121.4 188.8 %all-gather.2.cloned.1.call-start = ((), (), s32[]{:S(2)}) async-start(), calls=%async_computation.2 | async-start | bytes 4456448 | tf_op jit(solution)/shard_map/all_gather | solution.py:52
  237.2 297.8 %reduce-scatter.9.cloned.1.call-start = ((), (), s32[]{:S(2)}) async-start(), calls=%async_computation.4 | async-start | bytes 4456448
  310.1 3.4 copy-start.2
Sparse Core Ops, SparseCore 0:
  121.5 109.4 reduce-scatter.6
  237.3 72.7 all-gather.1
  428.9 105.9 reduce-scatter.8
where the time goes:
time: 556 us; the launch traced here: 548 us
  blocking collectives  234 us (42%)
  waiting for transfers between devices  190 us (34%)
  matrix products  60.7 us (11%)
  local copies, waits for them, and re-layouts  26.4 us (5%)
  other arithmetic  22.2 us (4%)
  between operations  14.3 us (3%)
    unnamed x5, waiting for transfers between devices  118 us
    psum x2, blocking collectives, count_sum(): return lax.psum(jnp.sum(weights, axis=0), 'pts')  85.5 us
    psum x2, blocking collectives, soft_weights(): total = lax.psum(jnp.sum(expo, axis=1, keepdims=True), 'cen')  76.7 us
    all_gather x1, waiting for transfers between devices, local(): piece = lax.all_gather(share, 'pts', axis=0, tiled=True)  72.7 us
    pmax x2, blocking collectives, soft_weights(): top = lax.pmax(local_top, 'cen')  71.6 us
    dot_general x2, matrix products, moment_share(): lax.dot_general(sample_vectors, weights, (((0,), (0,)), ((), ())), precis...  27.2 us
    unnamed x13, local copies, waits for them, and re-layouts  23.5 us
    dot_general x1, matrix products, local(): jnp.dot(sample_vectors, piece, precision=high, preferred_element_type=jnp...  21.7 us
  transfers between devices with their start and end apart: 3, of which 3 were waited for; matrix products, arithmetic and copies ran while one was open for 2% of the time, Pallas kernels for 0%

commit v1 on v0

v1 whole, which is shorter than its diff:
```python
import functools

import jax
import jax.numpy as jnp
from jax import lax
from jax.experimental import pallas as pl
from jax.experimental.pallas import tpu as pltpu
from jax.sharding import PartitionSpec as P

F32 = jnp.float32
BF16 = jnp.bfloat16
PAD = 8
MIB = 1 << 20
CORE, XA, XB, ZG = 1, 2, 6, 8
UNITS = ((0.5, (CORE, XA, XB, ZG)), (0.5, (CORE, XB, XA, ZG)))


def split(v):
    hi = v.astype(BF16)
    return hi, (v - hi.astype(F32)).astype(BF16)


def dot3(ah, al, bh, bl):
    dot = functools.partial(jnp.dot, preferred_element_type=F32)
    return dot(ah, bh) + (dot(ah, bl) + dot(al, bh))


def relative_blocks(gens):
    out = [0]
    for g in reversed(gens):
        out = out + [r ^ g for r in out]
    return out


def swap(v, g):
    return lax.ppermute(v, "pts", [(i, i ^ g) for i in range(lax.axis_size("pts"))])


def params(mib):
    return pltpu.CompilerParams(vmem_limit_bytes=mib * MIB)


def cost(flops, nbytes):
    return pl.CostEstimate(flops=int(flops), bytes_accessed=int(nbytes), transcendentals=0)


def softmax_part(raw, half_norm, e_ref, stat_ref):
    logits = (raw - half_norm) * 10.0
    top = jnp.max(logits, axis=1, keepdims=True)
    expo = jnp.exp(logits - top)
    total = jnp.sum(expo, axis=1, keepdims=True)
    e_ref[...] = expo
    rows = raw.shape[0]
    stat_ref[0:1, :] = jnp.broadcast_to(top, (rows, 128)).T[0:1, :]
    stat_ref[1:2, :] = jnp.broadcast_to(total, (rows, 128)).T[0:1, :]


def first_kernel(x_ref, c_ref, e_ref, stat_ref, xh_ref, xl_ref, th_ref, tl_ref, ch, cl, norm):
    @pl.when(pl.program_id(0) == 0)
    def _():
        c = c_ref[...]
        ch[...], cl[...] = split(c)
        norm[0:1, :] = 0.5 * jnp.sum(c * c, axis=0, keepdims=True)

    x = x_ref[...]
    xh, xl = split(x)
    xh_ref[...] = xh
    xl_ref[...] = xl
    th_ref[...], tl_ref[...] = split(x.T)
    softmax_part(dot3(xh, xl, ch[...], cl[...]), norm[0:1, :], e_ref, stat_ref)


def first_step(x, c, tile=256):
    n, d = x.shape
    k = c.shape[1]
    return pl.pallas_call(
        first_kernel,
        grid=(n // tile,),
        in_specs=[
            pl.BlockSpec((tile, d), lambda i: (i, 0)),
            pl.BlockSpec((d, k), lambda i: (0, 0)),
        ],
        out_specs=[
            pl.BlockSpec((tile, k), lambda i: (i, 0)),
            pl.BlockSpec((2, tile), lambda i: (0, i)),
            pl.BlockSpec((tile, d), lambda i: (i, 0)),
            pl.BlockSpec((tile, d), lambda i: (i, 0)),
            pl.BlockSpec((d, tile), lambda i: (0, i)),
            pl.BlockSpec((d, tile), lambda i: (0, i)),
        ],
        out_shape=[
            jax.ShapeDtypeStruct((n, k), F32),
            jax.ShapeDtypeStruct((2, n), F32),
            jax.ShapeDtypeStruct((n, d), BF16),
            jax.ShapeDtypeStruct((n, d), BF16),
            jax.ShapeDtypeStruct((d, n), BF16),
            jax.ShapeDtypeStruct((d, n), BF16),
        ],
        scratch_shapes=[
            pltpu.VMEM((d, k), BF16),
            pltpu.VMEM((d, k), BF16),
            pltpu.VMEM((8, k), F32),
        ],
        compiler_params=params(48),
        cost_estimate=cost(6 * n * d * k, 4 * (2 * n * d + d * k + n * k)),
        name="first_logits",
    )(x, c)


def next_kernel(layout, me_ref, *refs):
    n_in = 2 * len(layout)
    pieces = refs[:n_in]
    xh_ref, xl_ref, e_ref, stat_ref, ch, cl, norm = refs[n_in:]

    @pl.when(pl.program_id(0) == 0)
    def _():
        me = me_ref[0]
        for u, (start, width, order) in enumerate(layout):
            cols = slice(start, start + width)
            half = len(order) // 2
            rows = pieces[2 * u].shape[0] // half
            total = jnp.zeros((1, width), F32)
            for j, r in enumerate(order):
                piece = pieces[2 * u + j // half]
                v = piece[(j % half) * rows : (j % half + 1) * rows, :]
                hi, lo = split(v)
                at = pl.ds(pl.multiple_of((me ^ r) * rows, rows), rows)
                ch[at, cols] = hi
                cl[at, cols] = lo
                total = total + jnp.sum(v * v, axis=0, keepdims=True)
            norm[0:1, cols] = 0.5 * total

    softmax_part(
        dot3(xh_ref[...], xl_ref[...], ch[...], cl[...]), norm[0:1, :], e_ref, stat_ref
    )


def next_step(me, pieces, layout, xh, xl, tile=256):
    n, d = xh.shape
    k = sum(width for _, width, _ in layout)
    flat = [p for pair in pieces for p in pair]
    return pl.pallas_call(
        functools.partial(next_kernel, layout),
        grid=(n // tile,),
        in_specs=[pl.BlockSpec(memory_space=pltpu.SMEM)]
        + [pl.BlockSpec(p.shape, lambda i: (0, 0)) for p in flat]
        + [pl.BlockSpec((tile, d), lambda i: (i, 0))] * 2,
        out_specs=[
            pl.BlockSpec((tile, k), lambda i: (i, 0)),
            pl.BlockSpec((2, tile), lambda i: (0, i)),
        ],
        out_shape=[
            jax.ShapeDtypeStruct((n, k), F32),
            jax.ShapeDtypeStruct((2, n), F32),
        ],
        scratch_shapes=[
            pltpu.VMEM((d, k), BF16),
            pltpu.VMEM((d, k), BF16),
            pltpu.VMEM((8, k), F32),
        ],
        compiler_params=params(48),
        cost_estimate=cost(6 * n * d * k, 4 * (n * d + d * k + n * k)),
        name="next_logits",
    )(me, *flat, xh, xl)


def row_scale(own, everyone):
    tops = everyone[:, 0, :]
    top = jnp.max(tops, axis=0, keepdims=True)
    total = jnp.sum(everyone[:, 1, :] * jnp.exp(tops - top), axis=0, keepdims=True)
    return jnp.exp(own[0:1, :] - top) / total


def moment_kernel(order, me_ref, own_ref, all_ref, th_ref, tl_ref, e_ref, keep_ref, send_ref, ph, pt):
    me = me_ref[0]
    rows = th_ref.shape[0] // len(order)
    for j, r in enumerate(order):
        at = pl.ds(pl.multiple_of((me ^ r) * rows, rows), rows)
        ph[j * rows : (j + 1) * rows, :] = th_ref[at, :]
        pt[j * rows : (j + 1) * rows, :] = tl_ref[at, :]
    scale = row_scale(own_ref[...], all_ref[...])
    n = scale.shape[1]
    column = jnp.broadcast_to(scale, (128, n)).T[:, 0:1]
    w = e_ref[...] * column
    wh, wl = split(w)
    m = dot3(ph[...], pt[...], wh, wl)
    half = m.shape[0] // 2
    mass = jnp.broadcast_to(jnp.sum(w, axis=0, keepdims=True), (PAD, w.shape[1]))
    keep_ref[0:half, :] = m[:half]
    send_ref[0:half, :] = m[half:]
    keep_ref[half : half + PAD, :] = mass
    send_ref[half : half + PAD, :] = mass


def moment_step(me, own, everyone, th, tl, e, start, width, order):
    d, n = th.shape
    shape = jax.ShapeDtypeStruct((d // 2 + PAD, width), F32)
    whole = lambda a: pl.BlockSpec(a.shape, lambda i: (0,) * a.ndim)
    col = start // width
    return pl.pallas_call(
        functools.partial(moment_kernel, order),
        grid=(1,),
        in_specs=[
            pl.BlockSpec(memory_space=pltpu.SMEM),
            whole(own),
            whole(everyone),
            whole(th),
            whole(tl),
            pl.BlockSpec((n, width), lambda i: (0, col)),
        ],
        out_specs=[whole(shape), whole(shape)],
        out_shape=[shape, shape],
        scratch_shapes=[pltpu.VMEM((d, n), BF16), pltpu.VMEM((d, n), BF16)],
        compiler_params=params(48),
        cost_estimate=cost(6 * d * n * width, 4 * (d * n + n * width + d * width)),
        name="moments",
    )(me, own, everyone, th, tl, e)


def fold_kernel(keep_ref, recv_ref, out_ref, send_ref):
    half = (keep_ref.shape[0] - PAD) // 2
    out_ref[0:half, :] = keep_ref[0:half, :] + recv_ref[0:half, :]
    send_ref[0:half, :] = keep_ref[half : 2 * half, :] + recv_ref[half : 2 * half, :]
    mass = keep_ref[2 * half :, :] + recv_ref[2 * half :, :]
    out_ref[half:, :] = mass
    send_ref[half:, :] = mass


def fold(keep, recv):
    rows = (keep.shape[0] - PAD) // 2 + PAD
    shape = jax.ShapeDtypeStruct((rows, keep.shape[1]), F32)
    return pl.pallas_call(
        fold_kernel,
        out_shape=[shape, shape],
        compiler_params=params(16),
        cost_estimate=cost(keep.size, 16 * keep.size),
        name="fold",
    )(keep, recv)


def update_kernel(parts, keep_ref, recv_ref, old_ref, out_ref):
    rows = keep_ref.shape[0] - PAD
    mass = keep_ref[rows : rows + 1, :] + recv_ref[rows : rows + 1, :] + 1.0
    block = rows // parts
    for i in range(parts):
        here = slice(i * block, (i + 1) * block)
        there = slice((parts - 1 - i) * block, (parts - i) * block)
        out_ref[here, :] = (keep_ref[here, :] + recv_ref[there, :] + old_ref[here, :]) / mass


def scatter(keep, send, gens):
    for g in gens[:-1]:
        keep, send = fold(keep, swap(send, g))
    return keep, send


def old_rows(c, me, start, width, last, rows):
    parts = [
        lax.dynamic_slice(c, ((me[0] ^ r) * rows, jnp.int32(start)), (rows, width))
        for r in (0, last)
    ]
    return jnp.concatenate(parts, axis=0)


def update(keep, recv, old, parts=1):
    return pl.pallas_call(
        functools.partial(update_kernel, parts),
        out_shape=jax.ShapeDtypeStruct(old.shape, F32),
        compiler_params=params(16),
        cost_estimate=cost(4 * old.size, 16 * old.size),
        name="update",
    )(keep, recv, old)


def everyone_stats(stats):
    size = lax.axis_size("cen")
    return lax.all_to_all(jnp.broadcast_to(stats[None], (size, *stats.shape)), "cen", 0, 0)


def local(x, c):
    me = lax.axis_index("pts").astype(jnp.int32).reshape(1)
    k = c.shape[1]
    rows = c.shape[0] // lax.axis_size("pts")
    layout, start = [], 0
    for share, gens in UNITS:
        width = int(k * share)
        layout.append((start, width, gens, relative_blocks(gens)))
        start += width

    e, stats, xh, xl, th, tl = first_step(x, c)
    everyone = everyone_stats(stats)
    moments = [
        moment_step(me, stats, everyone, th, tl, e, s, w, order) for s, w, _, order in layout
    ]
    shares, pieces = [], []
    for (s, w, gens, order), (keep, send) in zip(layout, moments):
        old = old_rows(c, me, s, w, gens[-1], rows)
        for g in gens[:-2]:
            keep, send = fold(keep, swap(send, g))
        whole = join(keep, swap(send, gens[-2]))
        share = update(whole, swap(whole, gens[-1]), old, 2)
        shares.append(share)
        cur = share
        for g in gens[-2:0:-1]:
            cur = jnp.concatenate([cur, swap(cur, g)], axis=0)
        pieces.append((cur, swap(cur, gens[0])))

    plan = [(s, w, order) for s, w, _, order in layout]
    e, stats = next_step(me, pieces, plan, xh, xl)
    everyone = everyone_stats(stats)
    outs = []
    for (s, w, gens, order), share in zip(layout, shares):
        keep, send = moment_step(me, stats, everyone, th, tl, e, s, w, order)
        keep, send = scatter(keep, send, gens)
        outs.append(update(keep, swap(send, gens[-1]), share[:rows]))
    weights = e * row_scale(stats, everyone).reshape(-1, 1)
    return weights, jnp.concatenate(outs, axis=1)


def join_kernel(keep_ref, recv_ref, out_ref):
    out_ref[...] = keep_ref[...] + recv_ref[...]


def join(keep, recv):
    return pl.pallas_call(
        join_kernel,
        out_shape=jax.ShapeDtypeStruct(keep.shape, F32),
        compiler_params=params(16),
        cost_estimate=cost(keep.size, 12 * keep.size),
        name="join",
    )(keep, recv)


def solution(mesh):
    placed = (P("pts", None), P(None, "cen"))
    return jax.shard_map(
        local,
        mesh=mesh,
        in_specs=placed,
        out_specs=(P("pts", "cen"), P("pts", "cen")),
        check_vma=False,
    )
```

time: 556 us -> 192 us (0.35); the launches traced: 548 us -> 191 us
  blocking collectives: 234 us -> 12.5 us
  waiting for transfers between devices: 190 us -> 87 us
  matrix products: 60.7 us -> 0 us
  starting transfers between devices: 0.29 us -> 43.9 us
  Pallas kernels: 0 us -> 37.9 us
  local copies, waits for them, and re-layouts: 26.4 us -> 5.54 us
  other arithmetic: 22.2 us -> 3.05 us
  between operations: 14.3 us -> 0.87 us
    psum x4 -> x0, blocking collectives: 162 us -> none  [the longest x2 85.5 us: count_sum(): return lax.psum(jnp.sum(weights, axis=0), 'pts')]
    unnamed x5 -> x0, waiting for transfers between devices: 118 us -> none
    ppermute x0 -> x22, waiting for transfers between devices: none -> 80.1 us  [swap(): lax.ppermute(v, 'pts', [(i, i ^ g) for i in range(lax.axis_size('pts'))])]
    all_gather x1 -> x0, waiting for transfers between devices: 72.7 us -> none  [local(): piece = lax.all_gather(share, 'pts', axis=0, tiled=True)]
    pmax x2 -> x0, blocking collectives: 71.6 us -> none  [soft_weights(): top = lax.pmax(local_top, 'cen')]
    dot_general x4 -> x0, matrix products: 60.7 us -> none  [the longest x2 27.2 us: moment_share(): lax.dot_general(sample_vectors, weights, (((0,), (0,)), ((), ())), precis...]
    pallas_call x0 -> x22, Pallas kernels: none -> 37.9 us  [the longest x4 17 us: moment_step(): pl.pallas_call(functools.partial(moment_kernel, order), grid=(1,), in_spe...]
    ppermute x0 -> x22, starting transfers between devices: none -> 34.9 us  [swap(): lax.ppermute(v, 'pts', [(i, i ^ g) for i in range(lax.axis_size('pts'))])]
  transfers between devices with their start and end apart: 3 -> 23, of which waited for: 3 -> 17; matrix products, arithmetic and copies ran while one was open for 2% -> 2% of each run, Pallas kernels for 0% -> 5%
where the time goes in v1:
time: 192 us; the launch traced here: 191 us
  waiting for transfers between devices  87 us (45%)
  starting transfers between devices  43.9 us (23%)
  Pallas kernels  37.9 us (20%)
  blocking collectives  12.5 us (7%)
  local copies, waits for them, and re-layouts  5.54 us (3%)
  other arithmetic  3.05 us (2%)
    ppermute x22, waiting for transfers between devices, swap(): lax.ppermute(v, 'pts', [(i, i ^ g) for i in range(lax.axis_size('pts'))])  80.1 us
    ppermute x22, starting transfers between devices, swap(): lax.ppermute(v, 'pts', [(i, i ^ g) for i in range(lax.axis_size('pts'))])  34.9 us
    pallas_call x4, Pallas kernels, moment_step(): pl.pallas_call(functools.partial(moment_kernel, order), grid=(1,), in_spe...  17 us
    all_to_all x1, blocking collectives, everyone_stats(): lax.all_to_all(jnp.broadcast_to(stats[None], (size, *stats.shape)), 'cen'...  12.5 us
    pallas_call x1, Pallas kernels, first_step(): pl.pallas_call(first_kernel, grid=(n // tile,), in_specs=[pl.BlockSpec((t...  10.7 us
    pallas_call x1, Pallas kernels, next_step(): pl.pallas_call(functools.partial(next_kernel, layout), grid=(n // tile,),...  9.18 us
    all_to_all x1, starting transfers between devices, everyone_stats(): lax.all_to_all(jnp.broadcast_to(stats[None], (size, *stats.shape)), 'cen'...  8.99 us
    all_to_all x1, waiting for transfers between devices, everyone_stats(): lax.all_to_all(jnp.broadcast_to(stats[None], (size, *stats.shape)), 'cen'...  6.91 us
  transfers between devices with their start and end apart: 23, of which 17 were waited for; matrix products, arithmetic and copies ran while one was open for 2% of the time, Pallas kernels for 5%

profile of v1, /device:TPU:8, one launch (start us, length us, event | category | flops | bytes accessed | tf_op | source)
XLA Modules:
  0.0 190.8 jit_solution(8108440847478445425)
XLA Ops:
  0.6 10.7 %first_logits.1 = (f32[768,1024]{1,0:T(8,128)}, f32[2,768]{1,0:T(2,128)S(1)}, bf16[768,1024]{1,0:T(8,128)(2,1)S(1)}, bf16[768,1024]{1,0:T(8,128)(2,1)S(1)}, bf16...) custom-call(f32[768,1024]{1,0:T(8,128)} %x_ref.1, f32[1024,1024]{1,0:T(8,128)} %c_ref.1), custom_call_target="tpu_custom_call" | custom-call | flops 4831838208 | bytes 13631488 | tf_op jit(solution)/shard_map/first_logits/pallas_call | solution.py:76
  11.3 1.1 copy-done.3
  12.5 1.1 copy-done.5
  13.6 0.7 broadcast_in_dim.8
  14.3 9.0 %all-to-all-start = ((f32[16,2,768]{2,1,0:T(2,128)}), f32[16,2,768]{2,1,0:T(2,128)S(1)}, u32[]{:S(2)}, u32[]{:S(2)}) async-start(f32[16,2,768]{2,1,0:T(2,128)} %broadcast_in_dim.8), calls=%async_computation | async-start | bytes 196608 | tf_op jit(solution)/shard_map/all_to_all | solution.py:277
  23.3 6.9 %all-to-all-done.all_ref = f32[16,2,768]{2,1,0:T(2,128)S(1)} async-done(((f32[16,2,768]{2,1,0:T(2,128)}), f32[16,2,768]{2,1,0:T(2,128)S(1)}, u32[]{:S(2)}, u32[]{:S(2)}) %all-to-all-start) | async-done | bytes 98336 | tf_op jit(solution)/shard_map/all_to_all | solution.py:277
  30.2 1.4 copy-done
  31.6 4.3 %moments.5 = (f32[520,512]{1,0:T(8,128)S(1)}, f32[520,512]{1,0:T(8,128)S(1)}) custom-call(s32[1]{0:T(128)} %bitcast.me_ref, f32[2,768]{1,0:T(2,128)S(1)} %get-tuple-element.38.own_ref, f32[16,2,768]{2,1,0:T(2,128)S(1)} %all-to-all-done.all_ref, bf16[1024,768]{1,0:T(8,128)(2,1)S(1)} %get-tuple-element.39.th_ref, bf16[1024,768]{1,0:T(8,128)(2,1)S(1)} %copy-done, ...), custom_call_target="tpu_custom_call" | custom-call | flops 2415919104 | bytes 6815744 | tf_op jit(solution)/shard_map/moments/pallas_call | solution.py:200
  36.1 4.2 %moments.4 = (f32[520,512]{1,0:T(8,128)S(1)}, f32[520,512]{1,0:T(8,128)S(1)}) custom-call(s32[1]{0:T(128)} %bitcast.me_ref, f32[2,768]{1,0:T(2,128)S(1)} %get-tuple-element.38.own_ref, f32[16,2,768]{2,1,0:T(2,128)S(1)} %all-to-all-done.all_ref, bf16[1024,768]{1,0:T(8,128)(2,1)S(1)} %get-tuple-element.39.th_ref, bf16[1024,768]{1,0:T(8,128)(2,1)S(1)} %copy-done.1, ...), custom_call_target="tpu_custom_call" | custom-call | flops 2415919104 | bytes 6815744 | tf_op jit(solution)/shard_map/moments/pallas_call | solution.py:200
  40.3 0.6 collective-permute-start
  41.0 2.8 %collective-permute-start.8 = (f32[264,512]{1,0:T(8,128)S(1)}, f32[264,512]{1,0:T(8,128)S(1)}, u32[]{:S(2)}, u32[]{:S(2)}) collective-permute-start(f32[264,512]{1,0:T(8,128)S(1)} %get-tuple-element.51), channel_id=1, source_target_pairs={{0,96},{16,112},{32,64},{48,80},{64,32},{80,48},{96,0},{112,16},{1... | collective-permute-start | bytes 1622024 | tf_op jit(solution)/shard_map/ppermute | solution.py:36
  43.9 0.9 collective-permute-start.1
  44.9 11.6 %collective-permute-done.8.recv_ref = f32[264,512]{1,0:T(8,128)S(1)} collective-permute-done((f32[264,512]{1,0:T(8,128)S(1)}, f32[264,512]{1,0:T(8,128)S(1)}, u32[]{:S(2)}, u32[]{:S(2)}) %collective-permute-start.8) | collective-permute-done | bytes 540704 | tf_op jit(solution)/shard_map/ppermute | solution.py:36
  56.9 1.1 collective-permute-done.1.recv_ref
  58.0 2.8 %collective-permute-start.2 = (f32[136,512]{1,0:T(8,128)S(1)}, f32[136,512]{1,0:T(8,128)S(1)}, u32[]{:S(2)}, u32[]{:S(2)}) collective-permute-start(f32[136,512]{1,0:T(8,128)S(1)} %get-tuple-element.47), channel_id=1, source_target_pairs={{0,96},{16,112},{32,64},{48,80},{64,32},{80,48},{96,0},{112,16},{1... | collective-permute-start | bytes 835592 | tf_op jit(solution)/shard_map/ppermute | solution.py:36
  60.8 3.5 %collective-permute-done.9.recv_ref = f32[136,512]{1,0:T(8,128)S(1)} collective-permute-done((f32[136,512]{1,0:T(8,128)S(1)}, f32[136,512]{1,0:T(8,128)S(1)}, u32[]{:S(2)}, u32[]{:S(2)}) %collective-permute-start.9) | collective-permute-done | bytes 278560 | tf_op jit(solution)/shard_map/ppermute | solution.py:36
  64.4 4.6 %collective-permute-start.10 = (f32[136,512]{1,0:T(8,128)S(1)}, f32[136,512]{1,0:T(8,128)S(1)}, u32[]{:S(2)}, u32[]{:S(2)}) collective-permute-start(f32[136,512]{1,0:T(8,128)S(1)} %join.3.keep_ref), channel_id=1, source_target_pairs={{0,128},{16,144},{32,160},{48,176},{64,192},{80,208},{96,224},{112... | collective-permute-start | bytes 835592 | tf_op jit(solution)/shard_map/ppermute | solution.py:36
  69.0 2.8 %collective-permute-start.3 = (f32[136,512]{1,0:T(8,128)S(1)}, f32[136,512]{1,0:T(8,128)S(1)}, u32[]{:S(2)}, u32[]{:S(2)}) collective-permute-start(f32[136,512]{1,0:T(8,128)S(1)} %join.2.keep_ref), channel_id=1, source_target_pairs={{0,128},{16,144},{32,160},{48,176},{64,192},{80,208},{96,224},{112... | collective-permute-start | bytes 835592 | tf_op jit(solution)/shard_map/ppermute | solution.py:36
  71.8 1.1 constant_dynamic-slice_fusion.1
  73.0 13.3 %collective-permute-done.10.recv_ref = f32[136,512]{1,0:T(8,128)S(1)} collective-permute-done((f32[136,512]{1,0:T(8,128)S(1)}, f32[136,512]{1,0:T(8,128)S(1)}, u32[]{:S(2)}, u32[]{:S(2)}) %collective-permute-start.10) | collective-permute-done | bytes 278560 | tf_op jit(solution)/shard_map/ppermute | solution.py:36
  86.3 1.7 collective-permute-start.11
  88.1 5.2 %collective-permute-done.3.recv_ref = f32[136,512]{1,0:T(8,128)S(1)} collective-permute-done((f32[136,512]{1,0:T(8,128)S(1)}, f32[136,512]{1,0:T(8,128)S(1)}, u32[]{:S(2)}, u32[]{:S(2)}) %collective-permute-start.3) | collective-permute-done | bytes 278560 | tf_op jit(solution)/shard_map/ppermute | solution.py:36
  93.3 2.9 %collective-permute-start.4 = (f32[128,512]{1,0:T(8,128)S(1)}, f32[128,512]{1,0:T(8,128)S(1)}, u32[]{:S(2)}, u32[]{:S(2)}) collective-permute-start(f32[128,512]{1,0:T(8,128)S(1)} %update.4), channel_id=1, source_target_pairs={{0,96},{16,112},{32,64},{48,80},{64,32},{80,48},{96,0},{112,16},{1... | collective-permute-start | bytes 786440 | tf_op jit(solution)/shard_map/ppermute | solution.py:36
  96.2 0.6 collective-permute-start.12
  96.8 7.1 %collective-permute-done.4 = f32[128,512]{1,0:T(8,128)S(1)} collective-permute-done((f32[128,512]{1,0:T(8,128)S(1)}, f32[128,512]{1,0:T(8,128)S(1)}, u32[]{:S(2)}, u32[]{:S(2)}) %collective-permute-start.4) | collective-permute-done | bytes 262176 | tf_op jit(solution)/shard_map/ppermute | solution.py:36
  103.9 0.6 collective-permute-start.5
  104.5 6.7 %collective-permute-done.12 = f32[256,512]{1,0:T(8,128)S(1)} collective-permute-done((f32[256,512]{1,0:T(8,128)S(1)}, f32[256,512]{1,0:T(8,128)S(1)}, u32[]{:S(2)}, u32[]{:S(2)}) %collective-permute-start.12) | collective-permute-done | bytes 524320 | tf_op jit(solution)/shard_map/ppermute | solution.py:36
  111.4 1.7 collective-permute-done.5
  113.3 0.7 collective-permute-done.13.refs_3_
  114.1 1.9 collective-permute-done.6.refs_1_
  116.0 9.2 %next_logits.1 = (f32[768,1024]{1,0:T(8,128)}, f32[2,768]{1,0:T(2,128)S(1)}) custom-call(s32[1]{0:T(128)} %bitcast.me_ref, f32[512,512]{1,0:T(8,128)S(1)} %pad_maximum_fusion.refs_0_, f32[512,512]{1,0:T(8,128)S(1)} %collective-permute-done.6.refs_1_, f32[512,512]{1,0:T(8,128)S(1)} %pad_maximum_fusion.1.refs_2_, ...), custom_call_target="tpu_custom_call" | custom-call | flops 4831838208 | bytes 10485760 | tf_op jit(solution)/shard_map/next_logits/pallas_call | solution.py:142
  125.2 12.5 %all_to_all.10.all_ref = f32[16,2,768]{2,1,0:T(2,128)S(1)} all-to-all(f32[16,2,768]{2,1,0:T(2,128)S(1)} %broadcast_in_dim.9), channel_id=1, replica_groups=mesh['pts'=16,'cen'=16] {'cen'}, dimensions={0} | all-to-all | bytes 196608 | tf_op jit(solution)/shard_map/all_to_all | solution.py:277
  137.7 4.2 %moments.6 = (f32[520,512]{1,0:T(8,128)S(1)}, f32[520,512]{1,0:T(8,128)S(1)}) custom-call(s32[1]{0:T(128)} %bitcast.me_ref, f32[2,768]{1,0:T(2,128)S(1)} %get-tuple-element.57.own_ref, f32[16,2,768]{2,1,0:T(2,128)S(1)} %all_to_all.10.all_ref, bf16[1024,768]{1,0:T(8,128)(2,1)S(1)} %get-tuple-element.39.th_ref, bf16[1024,768]{1,0:T(8,128)(2,1)S(1)} %copy-done.2, ...), custom_call_target="tpu_custom_call" | custom-call | flops 2415919104 | bytes 6815744 | tf_op jit(solution)/shard_map/moments/pallas_call | solution.py:200
  142.1 4.2 %moments.7 = (f32[520,512]{1,0:T(8,128)S(1)}, f32[520,512]{1,0:T(8,128)S(1)}) custom-call(s32[1]{0:T(128)} %bitcast.me_ref, f32[2,768]{1,0:T(2,128)S(1)} %get-tuple-element.57.own_ref, f32[16,2,768]{2,1,0:T(2,128)S(1)} %all_to_all.10.all_ref, bf16[1024,768]{1,0:T(8,128)(2,1)S(1)} %get-tuple-element.39.th_ref, bf16[1024,768]{1,0:T(8,128)(2,1)S(1)} %copy-done.2, ...), custom_call_target="tpu_custom_call" | custom-call | flops 2415919104 | bytes 6815744 | tf_op jit(solution)/shard_map/moments/pallas_call | solution.py:200
  146.3 0.6 collective-permute-start.18
  147.0 0.6 collective-permute-start.15
  147.7 1.6 collective-permute-done.18.recv_ref
  149.4 3.1 %collective-permute-start.19 = (f32[264,512]{1,0:T(8,128)S(1)}, f32[264,512]{1,0:T(8,128)S(1)}, u32[]{:S(2)}, u32[]{:S(2)}) collective-permute-start(f32[264,512]{1,0:T(8,128)S(1)} %get-tuple-element.69), channel_id=1, source_target_pairs={{0,96},{16,112},{32,64},{48,80},{64,32},{80,48},{96,0},{112,16},{1... | collective-permute-start | bytes 1622024 | tf_op jit(solution)/shard_map/ppermute | solution.py:36
  152.5 8.8 %collective-permute-done.15.recv_ref = f32[264,512]{1,0:T(8,128)S(1)} collective-permute-done((f32[264,512]{1,0:T(8,128)S(1)}, f32[264,512]{1,0:T(8,128)S(1)}, u32[]{:S(2)}, u32[]{:S(2)}) %collective-permute-start.15) | collective-permute-done | bytes 540704 | tf_op jit(solution)/shard_map/ppermute | solution.py:36
  161.4 2.9 %collective-permute-start.16 = (f32[136,512]{1,0:T(8,128)S(1)}, f32[136,512]{1,0:T(8,128)S(1)}, u32[]{:S(2)}, u32[]{:S(2)}) collective-permute-start(f32[136,512]{1,0:T(8,128)S(1)} %get-tuple-element.63), channel_id=1, source_target_pairs={{0,96},{16,112},{32,64},{48,80},{64,32},{80,48},{96,0},{112,16},{1... | collective-permute-start | bytes 835592 | tf_op jit(solution)/shard_map/ppermute | solution.py:36
  164.3 1.7 collective-permute-done.19.recv_ref
  166.3 5.1 %collective-permute-done.16.recv_ref = f32[136,512]{1,0:T(8,128)S(1)} collective-permute-done((f32[136,512]{1,0:T(8,128)S(1)}, f32[136,512]{1,0:T(8,128)S(1)}, u32[]{:S(2)}, u32[]{:S(2)}) %collective-permute-start.16) | collective-permute-done | bytes 278560 | tf_op jit(solution)/shard_map/ppermute | solution.py:36
  171.4 4.4 %collective-permute-start.17 = (f32[72,512]{1,0:T(8,128)S(1)}, f32[72,512]{1,0:T(8,128)S(1)}, u32[]{:S(2)}, u32[]{:S(2)}) collective-permute-start(f32[72,512]{1,0:T(8,128)S(1)} %get-tuple-element.65), channel_id=1, source_target_pairs={{0,128},{16,144},{32,160},{48,176},{64,192},{80,208},{96,224},{112... | collective-permute-start | bytes 442376 | tf_op jit(solution)/shard_map/ppermute | solution.py:36
  175.8 2.3 %collective-permute-start.21 = (f32[72,512]{1,0:T(8,128)S(1)}, f32[72,512]{1,0:T(8,128)S(1)}, u32[]{:S(2)}, u32[]{:S(2)}) collective-permute-start(f32[72,512]{1,0:T(8,128)S(1)} %get-tuple-element.73), channel_id=1, source_target_pairs={{0,128},{16,144},{32,160},{48,176},{64,192},{80,208},{96,224},{112... | collective-permute-start | bytes 442376 | tf_op jit(solution)/shard_map/ppermute | solution.py:36
  178.1 1.9 %broadcast_multiply_fusion = f32[768,1024]{1,0:T(8,128)} fusion(f32[768,1024]{1,0:T(8,128)S(1)} %copy-done.6, f32[768]{0:T(1024)S(1)} %fusion.4), kind=kLoop, calls=%fused_computation | loop fusion | flops 786432 | bytes 6294528 | tf_op jit(solution)/shard_map/mul | solution.py:316
  180.0 7.4 %collective-permute-done.17.recv_ref = f32[72,512]{1,0:T(8,128)S(1)} collective-permute-done((f32[72,512]{1,0:T(8,128)S(1)}, f32[72,512]{1,0:T(8,128)S(1)}, u32[]{:S(2)}, u32[]{:S(2)}) %collective-permute-start.17) | collective-permute-done | bytes 147488 | tf_op jit(solution)/shard_map/ppermute | solution.py:36
  187.5 2.6 %collective-permute-done.21.recv_ref = f32[72,512]{1,0:T(8,128)S(1)} collective-permute-done((f32[72,512]{1,0:T(8,128)S(1)}, f32[72,512]{1,0:T(8,128)S(1)}, u32[]{:S(2)}, u32[]{:S(2)}) %collective-permute-start.21) | collective-permute-done | bytes 147488 | tf_op jit(solution)/shard_map/ppermute | solution.py:36
  190.1 0.7 pad_maximum_fusion.6
  (51 shorter events, 2.3 us)
Async XLA Ops:
  11.3 1.1 copy-start.3
  12.5 1.1 copy-start.5
  14.3 15.9 %all-to-all-start = ((f32[16,2,768]{2,1,0:T(2,128)}), f32[16,2,768]{2,1,0:T(2,128)S(1)}, u32[]{:S(2)}, u32[]{:S(2)}) async-start(f32[16,2,768]{2,1,0:T(2,128)} %broadcast_in_dim.8), calls=%async_computation | async-start | bytes 196608 | tf_op jit(solution)/shard_map/all_to_all | solution.py:277
  30.2 1.4 copy-start
  31.6 4.4 %copy-start.1 = (bf16[1024,768]{1,0:T(8,128)(2,1)S(1)}, bf16[1024,768]{1,0:T(8,128)(2,1)}, u32[]{:S(2)}) copy-start(bf16[1024,768]{1,0:T(8,128)(2,1)} %get-tuple-element.40.tl_ref) | copy-start | bytes 4718596
  35.9 4.9 %collective-permute-start.7 = (f32[520,512]{1,0:T(8,128)S(1)}, f32[520,512]{1,0:T(8,128)S(1)}, u32[]{:S(2)}, u32[]{:S(2)}) collective-permute-start(f32[520,512]{1,0:T(8,128)S(1)} %get-tuple-element.49), channel_id=1, source_target_pairs={{0,16},{16,0},{32,48},{48,32},{64,80},{80,64},{96,112},{112,96},{1... | collective-permute-start | bytes 3194888 | tf_op jit(solution)/shard_map/ppermute | solution.py:36
  40.3 3.5 %collective-permute-start = (f32[520,512]{1,0:T(8,128)S(1)}, f32[520,512]{1,0:T(8,128)S(1)}, u32[]{:S(2)}, u32[]{:S(2)}) collective-permute-start(f32[520,512]{1,0:T(8,128)S(1)} %get-tuple-element.43), channel_id=1, source_target_pairs={{0,16},{16,0},{32,48},{48,32},{64,80},{80,64},{96,112},{112,96},{1... | collective-permute-start | bytes 3194888 | tf_op jit(solution)/shard_map/ppermute | solution.py:36
  41.0 15.5 %collective-permute-start.8 = (f32[264,512]{1,0:T(8,128)S(1)}, f32[264,512]{1,0:T(8,128)S(1)}, u32[]{:S(2)}, u32[]{:S(2)}) collective-permute-start(f32[264,512]{1,0:T(8,128)S(1)} %get-tuple-element.51), channel_id=1, source_target_pairs={{0,96},{16,112},{32,64},{48,80},{64,32},{80,48},{96,0},{112,16},{1... | collective-permute-start | bytes 1622024 | tf_op jit(solution)/shard_map/ppermute | solution.py:36
  43.9 14.0 %collective-permute-start.1 = (f32[264,512]{1,0:T(8,128)S(1)}, f32[264,512]{1,0:T(8,128)S(1)}, u32[]{:S(2)}, u32[]{:S(2)}) collective-permute-start(f32[264,512]{1,0:T(8,128)S(1)} %get-tuple-element.45), channel_id=1, source_target_pairs={{0,32},{16,48},{32,0},{48,16},{64,96},{80,112},{96,64},{112,80},{1... | collective-permute-start | bytes 1622024 | tf_op jit(solution)/shard_map/ppermute | solution.py:36
  56.5 7.8 %collective-permute-start.9 = (f32[136,512]{1,0:T(8,128)S(1)}, f32[136,512]{1,0:T(8,128)S(1)}, u32[]{:S(2)}, u32[]{:S(2)}) collective-permute-start(f32[136,512]{1,0:T(8,128)S(1)} %get-tuple-element.53), channel_id=1, source_target_pairs={{0,32},{16,48},{32,0},{48,16},{64,96},{80,112},{96,64},{112,80},{1... | collective-permute-start | bytes 835592 | tf_op jit(solution)/shard_map/ppermute | solution.py:36
  58.0 11.0 %collective-permute-start.2 = (f32[136,512]{1,0:T(8,128)S(1)}, f32[136,512]{1,0:T(8,128)S(1)}, u32[]{:S(2)}, u32[]{:S(2)}) collective-permute-start(f32[136,512]{1,0:T(8,128)S(1)} %get-tuple-element.47), channel_id=1, source_target_pairs={{0,96},{16,112},{32,64},{48,80},{64,32},{80,48},{96,0},{112,16},{1... | collective-permute-start | bytes 835592 | tf_op jit(solution)/shard_map/ppermute | solution.py:36
  64.4 21.9 %collective-permute-start.10 = (f32[136,512]{1,0:T(8,128)S(1)}, f32[136,512]{1,0:T(8,128)S(1)}, u32[]{:S(2)}, u32[]{:S(2)}) collective-permute-start(f32[136,512]{1,0:T(8,128)S(1)} %join.3.keep_ref), channel_id=1, source_target_pairs={{0,128},{16,144},{32,160},{48,176},{64,192},{80,208},{96,224},{112... | collective-permute-start | bytes 835592 | tf_op jit(solution)/shard_map/ppermute | solution.py:36
  69.0 24.3 %collective-permute-start.3 = (f32[136,512]{1,0:T(8,128)S(1)}, f32[136,512]{1,0:T(8,128)S(1)}, u32[]{:S(2)}, u32[]{:S(2)}) collective-permute-start(f32[136,512]{1,0:T(8,128)S(1)} %join.2.keep_ref), channel_id=1, source_target_pairs={{0,128},{16,144},{32,160},{48,176},{64,192},{80,208},{96,224},{112... | collective-permute-start | bytes 835592 | tf_op jit(solution)/shard_map/ppermute | solution.py:36
  86.3 9.8 %collective-permute-start.11 = (f32[128,512]{1,0:T(8,128)S(1)}, f32[128,512]{1,0:T(8,128)S(1)}, u32[]{:S(2)}, u32[]{:S(2)}) collective-permute-start(f32[128,512]{1,0:T(8,128)S(1)} %update.5), channel_id=1, source_target_pairs={{0,32},{16,48},{32,0},{48,16},{64,96},{80,112},{96,64},{112,80},{1... | collective-permute-start | bytes 786440 | tf_op jit(solution)/shard_map/ppermute | solution.py:36
  93.3 10.5 %collective-permute-start.4 = (f32[128,512]{1,0:T(8,128)S(1)}, f32[128,512]{1,0:T(8,128)S(1)}, u32[]{:S(2)}, u32[]{:S(2)}) collective-permute-start(f32[128,512]{1,0:T(8,128)S(1)} %update.4), channel_id=1, source_target_pairs={{0,96},{16,112},{32,64},{48,80},{64,32},{80,48},{96,0},{112,16},{1... | collective-permute-start | bytes 786440 | tf_op jit(solution)/shard_map/ppermute | solution.py:36
  96.2 15.0 %collective-permute-start.12 = (f32[256,512]{1,0:T(8,128)S(1)}, f32[256,512]{1,0:T(8,128)S(1)}, u32[]{:S(2)}, u32[]{:S(2)}) collective-permute-start(f32[256,512]{1,0:T(8,128)S(1)} %pad_maximum_fusion.3), channel_id=1, source_target_pairs={{0,96},{16,112},{32,64},{48,80},{64,32},{80,48},{96,0},{112,16},{1... | collective-permute-start | bytes 1572872 | tf_op jit(solution)/shard_map/ppermute | solution.py:36
  103.9 9.3 %collective-permute-start.5 = (f32[256,512]{1,0:T(8,128)S(1)}, f32[256,512]{1,0:T(8,128)S(1)}, u32[]{:S(2)}, u32[]{:S(2)}) collective-permute-start(f32[256,512]{1,0:T(8,128)S(1)} %pad_maximum_fusion.2), channel_id=1, source_target_pairs={{0,32},{16,48},{32,0},{48,16},{64,96},{80,112},{96,64},{112,80},{1... | collective-permute-start | bytes 1572872 | tf_op jit(solution)/shard_map/ppermute | solution.py:36
  111.3 4.7 %copy-start.4 = (bf16[768,1024]{1,0:T(8,128)(2,1)S(1)}, bf16[768,1024]{1,0:T(8,128)(2,1)}, u32[]{:S(2)}) copy-start(bf16[768,1024]{1,0:T(8,128)(2,1)} %copy-done.3) | copy-start | bytes 4718596
  111.3 2.7 %collective-permute-start.13 = (f32[512,512]{1,0:T(8,128)S(1)}, f32[512,512]{1,0:T(8,128)S(1)}, u32[]{:S(2)}, u32[]{:S(2)}) collective-permute-start(f32[512,512]{1,0:T(8,128)S(1)} %pad_maximum_fusion.1.refs_2_), channel_id=1, source_target_pairs={{0,16},{16,0},{32,48},{48,32},{64,80},{80,64},{96,112},{112,96},{1... | collective-permute-start | bytes 3145736 | tf_op jit(solution)/shard_map/ppermute | solution.py:36
  113.2 2.7 %collective-permute-start.6 = (f32[512,512]{1,0:T(8,128)S(1)}, f32[512,512]{1,0:T(8,128)S(1)}, u32[]{:S(2)}, u32[]{:S(2)}) collective-permute-start(f32[512,512]{1,0:T(8,128)S(1)} %pad_maximum_fusion.refs_0_), channel_id=1, source_target_pairs={{0,16},{16,0},{32,48},{48,32},{64,80},{80,64},{96,112},{112,96},{1... | collective-permute-start | bytes 3145736 | tf_op jit(solution)/shard_map/ppermute | solution.py:36
  116.0 21.8 %copy-start.2 = (bf16[1024,768]{1,0:T(8,128)(2,1)S(1)}, bf16[1024,768]{1,0:T(8,128)(2,1)}, u32[]{:S(2)}) copy-start(bf16[1024,768]{1,0:T(8,128)(2,1)} %get-tuple-element.40.tl_ref) | copy-start | bytes 4718596
  142.0 4.9 %collective-permute-start.14 = (f32[520,512]{1,0:T(8,128)S(1)}, f32[520,512]{1,0:T(8,128)S(1)}, u32[]{:S(2)}, u32[]{:S(2)}) collective-permute-start(f32[520,512]{1,0:T(8,128)S(1)} %get-tuple-element.59), channel_id=1, source_target_pairs={{0,16},{16,0},{32,48},{48,32},{64,80},{80,64},{96,112},{112,96},{1... | collective-permute-start | bytes 3194888 | tf_op jit(solution)/shard_map/ppermute | solution.py:36
  146.3 2.9 %collective-permute-start.18 = (f32[520,512]{1,0:T(8,128)S(1)}, f32[520,512]{1,0:T(8,128)S(1)}, u32[]{:S(2)}, u32[]{:S(2)}) collective-permute-start(f32[520,512]{1,0:T(8,128)S(1)} %get-tuple-element.67), channel_id=1, source_target_pairs={{0,16},{16,0},{32,48},{48,32},{64,80},{80,64},{96,112},{112,96},{1... | collective-permute-start | bytes 3194888 | tf_op jit(solution)/shard_map/ppermute | solution.py:36
  147.0 14.3 %collective-permute-start.15 = (f32[264,512]{1,0:T(8,128)S(1)}, f32[264,512]{1,0:T(8,128)S(1)}, u32[]{:S(2)}, u32[]{:S(2)}) collective-permute-start(f32[264,512]{1,0:T(8,128)S(1)} %get-tuple-element.61), channel_id=1, source_target_pairs={{0,32},{16,48},{32,0},{48,16},{64,96},{80,112},{96,64},{112,80},{1... | collective-permute-start | bytes 1622024 | tf_op jit(solution)/shard_map/ppermute | solution.py:36
  149.4 16.6 %collective-permute-start.19 = (f32[264,512]{1,0:T(8,128)S(1)}, f32[264,512]{1,0:T(8,128)S(1)}, u32[]{:S(2)}, u32[]{:S(2)}) collective-permute-start(f32[264,512]{1,0:T(8,128)S(1)} %get-tuple-element.69), channel_id=1, source_target_pairs={{0,96},{16,112},{32,64},{48,80},{64,32},{80,48},{96,0},{112,16},{1... | collective-permute-start | bytes 1622024 | tf_op jit(solution)/shard_map/ppermute | solution.py:36
  161.3 16.8 %copy-start.6 = (f32[768,1024]{1,0:T(8,128)S(1)}, f32[768,1024]{1,0:T(8,128)}, u32[]{:S(2)}) copy-start(f32[768,1024]{1,0:T(8,128)} %get-tuple-element.56.e_ref) | copy-start | bytes 9437188
  161.4 10.0 %collective-permute-start.16 = (f32[136,512]{1,0:T(8,128)S(1)}, f32[136,512]{1,0:T(8,128)S(1)}, u32[]{:S(2)}, u32[]{:S(2)}) collective-permute-start(f32[136,512]{1,0:T(8,128)S(1)} %get-tuple-element.63), channel_id=1, source_target_pairs={{0,96},{16,112},{32,64},{48,80},{64,32},{80,48},{96,0},{112,16},{1... | collective-permute-start | bytes 835592 | tf_op jit(solution)/shard_map/ppermute | solution.py:36
  166.1 9.7 %collective-permute-start.20 = (f32[136,512]{1,0:T(8,128)S(1)}, f32[136,512]{1,0:T(8,128)S(1)}, u32[]{:S(2)}, u32[]{:S(2)}) collective-permute-start(f32[136,512]{1,0:T(8,128)S(1)} %get-tuple-element.71), channel_id=1, source_target_pairs={{0,32},{16,48},{32,0},{48,16},{64,96},{80,112},{96,64},{112,80},{1... | collective-permute-start | bytes 835592 | tf_op jit(solution)/shard_map/ppermute | solution.py:36
  171.4 16.0 %collective-permute-start.17 = (f32[72,512]{1,0:T(8,128)S(1)}, f32[72,512]{1,0:T(8,128)S(1)}, u32[]{:S(2)}, u32[]{:S(2)}) collective-permute-start(f32[72,512]{1,0:T(8,128)S(1)} %get-tuple-element.65), channel_id=1, source_target_pairs={{0,128},{16,144},{32,160},{48,176},{64,192},{80,208},{96,224},{112... | collective-permute-start | bytes 442376 | tf_op jit(solution)/shard_map/ppermute | solution.py:36
  175.8 14.2 %collective-permute-start.21 = (f32[72,512]{1,0:T(8,128)S(1)}, f32[72,512]{1,0:T(8,128)S(1)}, u32[]{:S(2)}, u32[]{:S(2)}) collective-permute-start(f32[72,512]{1,0:T(8,128)S(1)} %get-tuple-element.73), channel_id=1, source_target_pairs={{0,128},{16,144},{32,160},{48,176},{64,192},{80,208},{96,224},{112... | collective-permute-start | bytes 442376 | tf_op jit(solution)/shard_map/ppermute | solution.py:36

commit v2 on v0

v2 whole, which is shorter than its diff:
```python
import functools

import jax
import jax.numpy as jnp
from jax import lax
from jax.experimental import pallas as pl
from jax.experimental.pallas import tpu as pltpu
from jax.sharding import PartitionSpec as P

F32 = jnp.float32
BF16 = jnp.bfloat16
PAD = 8
MIB = 1 << 20
CORE, XA, XB, ZG = 1, 2, 6, 8
COST = 0.1
COLORS = ((CORE, XA, XB), (CORE, XB, XA))


def split(v):
    hi = v.astype(BF16)
    return hi, (v - hi.astype(F32)).astype(BF16)


def dot3(ah, al, bh, bl):
    dot = functools.partial(jnp.dot, preferred_element_type=F32)
    return dot(ah, bh) + (dot(ah, bl) + dot(al, bh))


def relative_blocks(gens):
    out = [0]
    for g in reversed(gens):
        out = out + [r ^ g for r in out]
    return out


def swap(v, g):
    return lax.ppermute(v, "pts", [(i, i ^ g) for i in range(lax.axis_size("pts"))])


def params(mib):
    return pltpu.CompilerParams(vmem_limit_bytes=mib * MIB)


def cost(flops, nbytes):
    return pl.CostEstimate(
        flops=int(flops * COST), bytes_accessed=int(nbytes * COST), transcendentals=0
    )


def far_memory(*arrays):
    out = [pltpu.with_memory_space_constraint(a, pltpu.HBM) for a in arrays]
    return out[0] if len(out) == 1 else out


def near_memory(*arrays):
    return [pltpu.with_memory_space_constraint(a, pltpu.VMEM) for a in arrays]


ANY = pl.BlockSpec(memory_space=pl.ANY)
SMALL = pl.BlockSpec(memory_space=pltpu.SMEM)
NEAR = pl.BlockSpec(memory_space=pltpu.VMEM)


def whole(a):
    return pl.BlockSpec(a.shape, lambda i, s: (0,) * len(a.shape))


def softmax_part(raw, half_norm, e_ref):
    logits = (raw - half_norm) * 10.0
    top = jnp.max(logits, axis=1, keepdims=True)
    expo = jnp.exp(logits - top)
    total = jnp.sum(expo, axis=1, keepdims=True)
    e_ref[...] = expo
    rows = raw.shape[0]
    row = lambda v: jnp.broadcast_to(v, (rows, 128)).T[0:1, :]
    return row(top), row(total)


def put_stats(stats, stat_ref, all_ref, at):
    for i, v in enumerate(stats):
        stat_ref[i : i + 1, at] = v
        all_ref[:, i : i + 1, at] = jnp.broadcast_to(v[None], (all_ref.shape[0], *v.shape))


def first_kernel(
    me_ref, at_ref, pin_ref, x_ref, c_ref, e_ref, stat_ref, all_ref, xh_ref, xl_ref, th_ref, tl_ref, ch, cl, norm
):
    @pl.when(pl.program_id(0) == 0)
    def _():
        c = c_ref[...]
        ch[...], cl[...] = split(c)
        norm[0:1, :] = 0.5 * jnp.sum(c * c, axis=0, keepdims=True)

    x = x_ref[...]
    xh, xl = split(x)
    xh_ref[...] = xh
    xl_ref[...] = xl
    th_ref[...], tl_ref[...] = split(x.T)
    stats = softmax_part(dot3(xh, xl, ch[...], cl[...]), norm[0:1, :], e_ref)
    put_stats(stats, stat_ref, all_ref, slice(None))


def first_step(me, at, pin, x, c, copies, tile=256):
    n, d = x.shape
    k = c.shape[1]
    return pl.pallas_call(
        first_kernel,
        grid=(n // tile,),
        in_specs=[
            SMALL,
            SMALL,
            ANY,
            pl.BlockSpec((tile, d), lambda i: (i, 0)),
            pl.BlockSpec((d, k), lambda i: (0, 0)),
        ],
        out_specs=[
            pl.BlockSpec((tile, k), lambda i: (i, 0)),
            pl.BlockSpec((2, tile), lambda i: (0, i)),
            pl.BlockSpec((copies, 2, tile), lambda i: (0, 0, i)),
            pl.BlockSpec((tile, d), lambda i: (i, 0)),
            pl.BlockSpec((tile, d), lambda i: (i, 0)),
            pl.BlockSpec((d, tile), lambda i: (0, i)),
            pl.BlockSpec((d, tile), lambda i: (0, i)),
        ],
        out_shape=[
            pltpu.VMEM((n, k), F32),
            jax.ShapeDtypeStruct((2, n), F32),
            jax.ShapeDtypeStruct((copies, 2, n), F32),
            pltpu.HBM((n, d), BF16),
            pltpu.HBM((n, d), BF16),
            pltpu.VMEM((d, n), BF16),
            pltpu.VMEM((d, n), BF16),
        ],
        scratch_shapes=[
            pltpu.VMEM((d, k), BF16),
            pltpu.VMEM((d, k), BF16),
            pltpu.VMEM((8, k), F32),
        ],
        compiler_params=params(36),
        cost_estimate=cost(20 * 6 * n * d * k, 4 * (2 * n * d + d * k + n * k)),
        name="first_logits",
    )(me, at, pin, *far_memory(x, c))


def far_kernel(at_ref, *refs):
    pieces, (xh_ref, xl_ref, th_ref, tl_ref) = refs[:4], refs[4:]
    width = pieces[0].shape[1]
    for shift, piece in enumerate(pieces):
        quarter = lax.rem(at_ref[3] - shift + 4, 4)
        at = pl.ds(pl.multiple_of(quarter * width, width), width)
        v = piece[...]
        xh_ref[:, at], xl_ref[:, at] = split(v)
        th_ref[at, :], tl_ref[at, :] = split(v.T)


def far_points(at, pieces):
    n, width = pieces[0].shape
    d = width * len(pieces)
    return pl.pallas_call(
        far_kernel,
        in_specs=[SMALL] + [NEAR] * len(pieces),
        out_specs=[NEAR] * 4,
        out_shape=[pltpu.VMEM(s, BF16) for s in ((n, d), (n, d), (d, n), (d, n))],
        compiler_params=params(16),
        cost_estimate=cost(4 * n * d, 12 * n * d),
        name="far_points",
    )(at, *pieces)


def slice_kernel(at_ref, pin_ref, x_ref, out_ref):
    out_ref[...] = x_ref[...]


def own_piece(x, at):
    n, size = x.shape[0], x.shape[1] // 8
    return pl.pallas_call(
        lambda at_ref, x_ref, out_ref: slice_kernel(at_ref, None, x_ref, out_ref),
        grid_spec=pltpu.PrefetchScalarGridSpec(
            num_scalar_prefetch=1,
            grid=(1,),
            in_specs=[pl.BlockSpec((n, size), lambda i, s: (0, s[0]))],
            out_specs=pl.BlockSpec((n, size), lambda i, s: (0, 0)),
        ),
        out_shape=jax.ShapeDtypeStruct((n, size), F32),
        compiler_params=params(8),
        cost_estimate=cost(1, 8 * n * size),
        name="own_piece",
    )(at, far_memory(x))


def couple_kernel(at_ref, pin_ref, mine_ref, other_ref, out_ref):
    width = mine_ref.shape[1]
    side = at_ref[0] & 1
    out_ref[:, pl.ds(pl.multiple_of(side * width, width), width)] = mine_ref[...]
    out_ref[:, pl.ds(pl.multiple_of((1 - side) * width, width), width)] = other_ref[...]


def couple(at, pin, mine, other):
    n, width = mine.shape
    return pl.pallas_call(
        couple_kernel,
        in_specs=[SMALL, ANY, NEAR, NEAR],
        out_specs=NEAR,
        out_shape=jax.ShapeDtypeStruct((n, 2 * width), F32),
        compiler_params=params(4),
        cost_estimate=cost(1, 16 * n * width),
        name="couple",
    )(at, pin, mine, other)


def old_block(c, me, rows, width, pin):
    return pl.pallas_call(
        slice_kernel,
        grid_spec=pltpu.PrefetchScalarGridSpec(
            num_scalar_prefetch=1,
            grid=(2,),
            in_specs=[
                ANY,
                pl.BlockSpec((rows, width), lambda b, s: ((s[0] & 7) + 8 * b, s[0] // 8)),
            ],
            out_specs=pl.BlockSpec((rows, width), lambda b, s: (b, 0)),
        ),
        out_shape=jax.ShapeDtypeStruct((2 * rows, width), F32),
        compiler_params=params(4),
        cost_estimate=cost(1, 16 * rows * width),
        name="old_block",
    )(me, pin, far_memory(c))


def spread(orders, me_ref, pieces, ch, cl, norm):
    low = me_ref[0] & 7
    width = pieces[0].shape[1]
    for u, order in enumerate(orders):
        cols = slice(u * width, (u + 1) * width)
        half = len(order) // 2
        rows = pieces[2 * u].shape[0] // half // 2
        total = jnp.zeros((1, width), F32)
        for j, r in enumerate(order):
            piece = pieces[2 * u + j // half]
            for b in range(2):
                start = ((j % half) * 2 + b) * rows
                v = piece[start : start + rows, :]
                hi, lo = split(v)
                at = pl.ds(pl.multiple_of(((low ^ r) + 8 * b) * rows, rows), rows)
                ch[at, cols] = hi
                cl[at, cols] = lo
                total = total + jnp.sum(v * v, axis=0, keepdims=True)
        norm[:, cols] = jnp.broadcast_to(0.5 * total, (8, width))


def own_kernel(orders, me_ref, *refs):
    pieces = refs[: 2 * len(orders)]
    xh_ref, xl_ref, e_ref, stat_ref, ch, cl, norm = refs[2 * len(orders) :]

    @pl.when(pl.program_id(0) == 0)
    def _():
        spread(orders, me_ref, pieces, ch, cl, norm)

    raw = dot3(xh_ref[...], xl_ref[...], ch[...], cl[...])
    top, total = softmax_part(raw, norm[0:1, :], e_ref)
    stat_ref[0:1, :] = top
    stat_ref[1:2, :] = total


def own_logits(me, pieces, orders, near, tile=256):
    n, d = near[0].shape
    k = sum(pair[0].shape[1] for pair in pieces)
    flat = [p for pair in pieces for p in pair]
    shapes = [pltpu.VMEM((d, k), BF16), pltpu.VMEM((d, k), BF16), pltpu.VMEM((8, k), F32)]
    return pl.pallas_call(
        functools.partial(own_kernel, orders),
        grid_spec=pltpu.PrefetchScalarGridSpec(
            num_scalar_prefetch=1,
            grid=(n // tile,),
            in_specs=[NEAR] * len(flat) + [pl.BlockSpec((tile, d), lambda i, s: (i, 0))] * 2,
            out_specs=[
                pl.BlockSpec((tile, k), lambda i, s: (i, 0)),
                pl.BlockSpec((2, tile), lambda i, s: (0, i)),
                NEAR,
                NEAR,
                NEAR,
            ],
        ),
        out_shape=[pltpu.VMEM((n, k), F32), jax.ShapeDtypeStruct((2, n), F32), *shapes],
        compiler_params=params(24),
        cost_estimate=cost(6 * n * d * k, 4 * (n * d + d * k + n * k)),
        name="own_logits",
    )(me, *flat, *far_memory(*near))


def far_logits_kernel(
    me_ref, ch, cl, norm, own_ref, xh_ref, xl_ref, e_ref, stat_ref
):
    step = pl.program_id(0)
    tile = e_ref.shape[0]
    n = own_ref.shape[1]
    z = me_ref[0] // 8
    raw = dot3(xh_ref[...], xl_ref[...], ch[...], cl[...])
    stats = softmax_part(raw, norm[0:1, :], e_ref)
    at = pl.ds(pl.multiple_of((1 - z) * n + step * tile, tile), tile)
    for i, v in enumerate(stats):
        stat_ref[i : i + 1, at] = v

    @pl.when(step == 0)
    def _():
        stat_ref[:, pl.ds(pl.multiple_of(z * n, n), n)] = own_ref[...]


def far_logits(me, ch, cl, norm, own, far, tile=256):
    n, d = far[0].shape
    k = ch.shape[1]
    return pl.pallas_call(
        far_logits_kernel,
        grid_spec=pltpu.PrefetchScalarGridSpec(
            num_scalar_prefetch=1,
            grid=(n // tile,),
            in_specs=[NEAR] * 4 + [pl.BlockSpec((tile, d), lambda i, s: (i, 0))] * 2,
            out_specs=[pl.BlockSpec((tile, k), lambda i, s: (i, 0)), NEAR],
        ),
        out_shape=[
            pltpu.VMEM((n, k), F32),
            jax.ShapeDtypeStruct((2, 2 * n), F32),
        ],
        compiler_params=params(24),
        cost_estimate=cost(6 * n * d * k, 4 * (n * d + d * k + n * k)),
        name="far_logits",
    )(me, ch, cl, norm, own, *far)


def merge_kernel(pin_ref, mine_ref, other_ref, out_ref):
    top = jnp.maximum(mine_ref[0:1, :], other_ref[0:1, :])
    total = sum(ref[1:2, :] * jnp.exp(ref[0:1, :] - top) for ref in (mine_ref, other_ref))
    for i, v in enumerate((top, total)):
        out_ref[:, i : i + 1, :] = jnp.broadcast_to(v[None], (out_ref.shape[0], *v.shape))


def merge(pin, mine, other, copies):
    return pl.pallas_call(
        merge_kernel,
        in_specs=[ANY, NEAR, NEAR],
        out_specs=NEAR,
        out_shape=jax.ShapeDtypeStruct((copies, *mine.shape), F32),
        compiler_params=params(4),
        cost_estimate=cost(copies * mine.size, 8 * copies * mine.size),
        name="merge",
    )(pin, mine, other)


def row_scale(own, everyone):
    tops = everyone[:, 0, :]
    top = jnp.max(tops, axis=0, keepdims=True)
    total = jnp.sum(everyone[:, 1, :] * jnp.exp(tops - top), axis=0, keepdims=True)
    scale = jnp.exp(own[0:1, :] - top) / total
    return jnp.broadcast_to(scale, (128, scale.shape[1])).T[:, 0:1]


def permuted(order, low, ref, out):
    rows = ref.shape[0] // (2 * len(order))
    for j, r in enumerate(order):
        for b in range(2):
            at = pl.ds(pl.multiple_of(((low ^ r) + 8 * b) * rows, rows), rows)
            out[(2 * j + b) * rows : (2 * j + b + 1) * rows, :] = ref[at, :]


def emit(m, w, keep_ref, send_ref, at):
    half = m.shape[0] // 2
    mass = jnp.broadcast_to(jnp.sum(w, axis=0, keepdims=True), (PAD, w.shape[1]))
    keep_ref[0:half, at] = m[:half]
    send_ref[0:half, at] = m[half:]
    keep_ref[half : half + PAD, at] = mass
    send_ref[half : half + PAD, at] = mass


def first_moment_kernel(
    order, color, me_ref, pin_ref, own_ref, all_ref, th_ref, tl_ref, e_ref, keep_ref, send_ref, ph, pt
):
    low, z = me_ref[0] & 7, me_ref[0] // 8
    permuted(order, low, th_ref, ph)
    permuted(order, low, tl_ref, pt)
    scale = row_scale(own_ref[...], all_ref[...])
    width = e_ref.shape[1] // 4
    for h in range(2):
        column = pl.multiple_of((2 * (z ^ h) + color) * width, width)
        w = e_ref[:, pl.ds(column, width)] * scale
        wh, wl = split(w)
        m = dot3(ph[...], pt[...], wh, wl)
        emit(m, w, keep_ref, send_ref, slice(h * width, (h + 1) * width))


def first_moments(me, pin, own, everyone, th, tl, e, color, order):
    d, n = th.shape
    width = e.shape[1] // 4
    shape = jax.ShapeDtypeStruct((d // 2 + PAD, 2 * width), F32)
    return pl.pallas_call(
        functools.partial(first_moment_kernel, order, color),
        in_specs=[SMALL, ANY] + [NEAR] * 5,
        out_specs=[NEAR, NEAR],
        out_shape=[shape, shape],
        scratch_shapes=[pltpu.VMEM((d, n), BF16), pltpu.VMEM((d, n), BF16)],
        compiler_params=params(20),
        cost_estimate=cost(12 * d * n * width, 4 * (d * n + 2 * n * width + 2 * d * width)),
        name="first_moments",
    )(me, pin, own, everyone, th, tl, e)


def next_moment_kernel(
    order, color, me_ref, pin_ref, own, everyone, oh, ol, gh, gl, e0, e1, keep_ref, send_ref, ph, pt
):
    low, z = me_ref[0] & 7, me_ref[0] // 8
    n = e0.shape[0]
    width = e0.shape[1] // 2
    m = w_all = None
    for h, (th, tl, e) in enumerate(((oh, ol, e0), (gh, gl, e1))):
        at = pl.ds(pl.multiple_of((z ^ h) * n, n), n)
        permuted(order, low, th, ph)
        permuted(order, low, tl, pt)
        w = e[:, color * width : (color + 1) * width] * row_scale(own[:, at], everyone[:, :, at])
        wh, wl = split(w)
        part = dot3(ph[...], pt[...], wh, wl)
        m, w_all = (part, w) if m is None else (m + part, w_all + w)
    emit(m, w_all, keep_ref, send_ref, slice(None))


def next_moments(me, pin, own, everyone, near, far, e_own, e_far, color, order):
    d, n = near[0].shape
    width = e_own.shape[1] // 2
    shape = jax.ShapeDtypeStruct((d // 2 + PAD, width), F32)
    return pl.pallas_call(
        functools.partial(next_moment_kernel, order, color),
        in_specs=[SMALL, ANY] + [NEAR] * 8,
        out_specs=[NEAR, NEAR],
        out_shape=[shape, shape],
        scratch_shapes=[pltpu.VMEM((d, n), BF16)] * 2,
        compiler_params=params(20),
        cost_estimate=cost(12 * d * n * width, 4 * (2 * d * n + 2 * n * width + d * width)),
        name="next_moments",
    )(me, pin, own, everyone, *near, *far, e_own, e_far)


def relay_kernel(pin_ref, in_ref, out_ref):
    pass


def relay(a, pin):
    return pl.pallas_call(
        relay_kernel,
        in_specs=[ANY, ANY],
        out_specs=ANY,
        out_shape=jax.ShapeDtypeStruct(a.shape, a.dtype),
        input_output_aliases={1: 0},
        compiler_params=params(4),
        cost_estimate=cost(1, 1),
        name="relay",
    )(pin, a)


def fold_kernel(pins, *refs):
    refs = refs[pins:]
    count = len(refs) // 4
    for u in range(count):
        keep, recv = refs[2 * u : 2 * u + 2]
        out, send = refs[2 * (count + u) : 2 * (count + u) + 2]
        half = (keep.shape[0] - PAD) // 2
        out[0:half, :] = keep[0:half, :] + recv[0:half, :]
        send[0:half, :] = keep[half : 2 * half, :] + recv[half : 2 * half, :]
        mass = keep[2 * half :, :] + recv[2 * half :, :]
        out[half:, :] = mass
        send[half:, :] = mass


def pairs(flat):
    return [(flat[2 * i], flat[2 * i + 1]) for i in range(len(flat) // 2)]


def chain(kernel, name, ins, shapes, pins=()):
    size = sum(a.size for a in ins)
    return pl.pallas_call(
        kernel,
        in_specs=[ANY] * len(pins) + [NEAR] * len(ins),
        out_shape=[jax.ShapeDtypeStruct(shape, F32) for shape in shapes],
        compiler_params=params(12),
        cost_estimate=cost(size, 8 * size),
        name=name,
    )(*pins, *ins)


def fold(ins, *pin):
    shapes = []
    for keep, _ in ins:
        shapes += [((keep.shape[0] - PAD) // 2 + PAD, keep.shape[1])] * 2
    return pairs(chain(
            functools.partial(fold_kernel, len(pin)),
            "fold",
            [a for pair in ins for a in pair],
            shapes,
            pin,
        ))


def part_kernel(pins, *refs):
    refs = refs[pins:]
    count = len(refs) // 4
    for u in range(count):
        keep, recv = refs[2 * u : 2 * u + 2]
        out, send = refs[2 * (count + u) : 2 * (count + u) + 2]
        half = keep.shape[1] // 2
        out[...] = keep[:, 0:half] + recv[:, 0:half]
        send[...] = keep[:, half:] + recv[:, half:]


def part(ins, *pin):
    shapes = []
    for keep, _ in ins:
        shapes += [(keep.shape[0], keep.shape[1] // 2)] * 2
    return pairs(
        chain(
            functools.partial(part_kernel, len(pin)),
            "part",
            [a for pair in ins for a in pair],
            shapes,
            pin,
        )
    )


def update_kernel(pins, *refs):
    refs = refs[pins:]
    count = (len(refs) - 2) // 3
    old, joint = refs[2 * count], refs[-1]
    for u in range(count):
        keep, recv = refs[2 * u : 2 * u + 2]
        rows, width = old.shape[0], keep.shape[1]
        mass = keep[rows : rows + 1, :] + recv[rows : rows + 1, :] + 1.0
        cols = slice(u * width, (u + 1) * width)
        new = (keep[0:rows, :] + recv[0:rows, :] + old[:, cols]) / mass
        refs[2 * count + 1 + u][...] = new
        joint[:, cols] = new


def update(ins, old, *pin):
    flat = [a for pair in ins for a in pair]
    shapes = [(old.shape[0], keep.shape[1]) for keep, _ in ins] + [old.shape]
    return chain(functools.partial(update_kernel, len(pin)), "update", flat + [old], shapes, pin)


def stack_kernel(pins, *refs):
    refs = refs[pins:]
    count = len(refs) // 3
    for u in range(count):
        own, other, out = refs[2 * u], refs[2 * u + 1], refs[2 * count + u]
        rows = own.shape[0]
        out[0:rows, :] = own[...]
        out[rows:, :] = other[...]


def stack(ins, *pin):
    shapes = [(2 * own.shape[0], own.shape[1]) for own, _ in ins]
    flat = [a for pair in ins for a in pair]
    return chain(functools.partial(stack_kernel, len(pin)), "stack", flat, shapes, pin)


def column_kernel(pin_ref, *refs):
    rows = refs[0].shape[0]
    for i, ref in enumerate(refs[:-1]):
        refs[-1][i * rows : (i + 1) * rows, :] = ref[...]


def column(pieces, pin):
    rows, width = pieces[0].shape
    return chain(column_kernel, "column", pieces, [(rows * len(pieces), width)], [pin])[0]


def last_kernel(me_ref, *refs):
    ins, (mine_ref, theirs_ref) = refs[:-2], refs[-2:]
    z = me_ref[0] // 8
    for u in range(len(ins) // 3):
        keep, recv, old = ins[3 * u : 3 * u + 3]
        rows, width = old.shape
        mass = keep[rows : rows + 1, :] + recv[rows : rows + 1, :] + 1.0
        for out, which in ((mine_ref, z), (theirs_ref, 1 - z)):
            at = pl.ds(pl.multiple_of(which * (rows // 2), rows // 2), rows // 2)
            out[:, u * width : (u + 1) * width] = (keep[at, :] + recv[at, :] + old[at, :]) / mass


def last_update(me, triples):
    rows, width = triples[0][2].shape
    shape = jax.ShapeDtypeStruct((rows // 2, width * len(triples)), F32)
    flat = [a for t in triples for a in t]
    return pl.pallas_call(
        last_kernel,
        in_specs=[pl.BlockSpec(memory_space=pltpu.SMEM)]
        + [pl.BlockSpec(memory_space=pltpu.VMEM)] * len(flat),
        out_specs=[pl.BlockSpec(memory_space=pltpu.VMEM)] * 2,
        out_shape=[shape, shape],
        compiler_params=params(12),
        cost_estimate=cost(8 * rows * width, 32 * rows * width),
        name="last_update",
    )(me, *flat)


def weights_kernel(
    me_ref,
    own_ref,
    all_ref,
    e_ref,
    xh_ref,
    xl_ref,
    mine_ref,
    other_ref,
    out_ref,
    tick_ref,
    ch,
    cl,
    norm,
):
    me = me_ref[0]
    core, z = me & 1, me // 8

    @pl.when(pl.program_id(0) == 0)
    def _():
        rows = mine_ref.shape[0] // 8
        total = jnp.zeros((1, mine_ref.shape[1]), F32)
        for piece, side in ((mine_ref, core), (other_ref, 1 - core)):
            for j in range(8):
                v = piece[j * rows : (j + 1) * rows, :]
                hi, lo = split(v)
                x = (((me >> 1) & 3) - j // 2 + 4) & 3
                block = x * 2 + side + 8 * (j % 2)
                at = pl.ds(pl.multiple_of(block * rows, rows), rows)
                ch[at, :] = hi
                cl[at, :] = lo
                total = total + jnp.sum(v * v, axis=0, keepdims=True)
        norm[0:1, :] = 0.5 * total

    tops = all_ref[:, 0, :]
    top = jnp.max(tops, axis=0, keepdims=True)
    total = jnp.sum(all_ref[:, 1, :] * jnp.exp(tops - top), axis=0, keepdims=True)
    width = e_ref.shape[1]
    column = lambda v: jnp.broadcast_to(v, (128, v.shape[1])).T[:, 0:1]
    here = pl.ds(pl.multiple_of(z * width, width), width)
    there = pl.ds(pl.multiple_of((1 - z) * width, width), width)
    out_ref[:, here] = e_ref[...] * column(jnp.exp(own_ref[0:1, :] - top) / total)
    raw = dot3(xh_ref[...], xl_ref[...], ch[...], cl[...])
    logits = (raw - norm[0:1, :]) * 10.0
    out_ref[:, there] = jnp.exp(logits - column(top)) * column(1.0 / total)
    tick_ref[...] = norm[:, 0:128]


def final_weights(me, own, everyone, e_own, near, mine, other, tile=256):
    n, width = e_own.shape
    d = near[0].shape[1]
    t = n // tile
    rows = pl.BlockSpec((tile, d), lambda i, s: (i, 0))
    return pl.pallas_call(
        weights_kernel,
        grid_spec=pltpu.PrefetchScalarGridSpec(
            num_scalar_prefetch=1,
            grid=(t,),
            in_specs=[
                pl.BlockSpec((2, tile), lambda i, s: (0, (s[0] // 8) * t + i)),
                pl.BlockSpec(
                    (everyone.shape[0], 2, tile), lambda i, s: (0, 0, (s[0] // 8) * t + i)
                ),
                pl.BlockSpec((tile, width), lambda i, s: (i, 0)),
                rows,
                rows,
                NEAR,
                NEAR,
            ],
            out_specs=[pl.BlockSpec((tile, 2 * width), lambda i, s: (i, 0)), NEAR],
            scratch_shapes=[
                pltpu.VMEM((d, width), BF16),
                pltpu.VMEM((d, width), BF16),
                pltpu.VMEM((8, width), F32),
            ],
        ),
        out_shape=[pltpu.HBM((n, 2 * width), F32), jax.ShapeDtypeStruct((8, 128), F32)],
        compiler_params=params(24),
        cost_estimate=cost(6 * n * width * d, 4 * (n * d + 3 * n * width + d * width)),
        name="weights",
    )(me, own, everyone, e_own, *far_memory(*near), mine, other)


def local(x, c):
    index = lax.axis_index("pts").astype(jnp.int32)
    me = index.reshape(1)
    place_cen = lax.axis_index("cen").astype(jnp.int32)
    run, y = place_cen & 3, place_cen // 4
    at = jnp.stack([y * 2 + (run & 1), run >> 1, run, y])
    d, k = c.shape
    rows = d // 16
    cen = lax.axis_size("cen")
    orders = [relative_blocks(gens) for gens in COLORS]
    along_y = lambda v, shift: lax.ppermute(
        v, "cen", [(j, (j + 4 * shift) % cen) for j in range(cen)]
    )

    piece = own_piece(x, at)
    e, stats, copies, xh, xl, th, tl = first_step(me, at, piece, x, c, cen)
    piece = swap(piece, ZG)
    everyone = lax.all_to_all(copies, "cen", 0, 0)
    units, pin = [], piece
    for u, order in enumerate(orders):
        units.append(first_moments(me, pin, stats, everyone, th, tl, e, u, order))
        pin = units[-1][1]
    old = old_block(c, me, rows, k // 2, pin)
    other = lax.ppermute(relay(piece, units[0][1]), "cen", [(j, j ^ 1) for j in range(cen)])
    quarter = couple(at, old, piece, other)
    units = fold([(k_, swap(s_, g[0])) for g, (k_, s_) in zip(COLORS, units)])
    units = fold([(k_, swap(s_, g[1])) for g, (k_, s_) in zip(COLORS, units)], quarter)
    quarters = [quarter] + [along_y(quarter, shift) for shift in (1, 2, 3)]
    units = part([(k_, swap(s_, g[2])) for g, (k_, s_) in zip(COLORS, units)])
    units = [(k_, swap(s_, ZG)) for k_, s_ in units]
    *shares, joint = update(units, old, quarters[1], quarters[3])
    joint = swap(joint, ZG)
    cur = stack([(v, swap(v, g[2])) for g, v in zip(COLORS, shares)], quarters[2])
    fh, fl, gh, gl = far_points(at, quarters)
    cur = stack([(v, swap(v, g[1])) for g, v in zip(COLORS, cur)])
    pieces = [(v, swap(v, CORE)) for v in cur]
    e_own, stats, ch, cl, norm = own_logits(me, pieces, orders, (xh, xl))
    e_far, stats = far_logits(me, ch, cl, norm, stats, (fh, fl))
    everyone = lax.all_to_all(merge(joint, stats, swap(stats, ZG), cen), "cen", 0, 0)
    joint = relay(joint, everyone)
    peers = [joint]
    for shift in (1, 2, 3):
        to = [(i, (i & 9) | ((((i >> 1) + shift) & 3) << 1)) for i in range(16)]
        peers.append(lax.ppermute(joint, "pts", to))
    units, pin = [], everyone
    for u, order in enumerate(orders):
        units.append(
            next_moments(me, pin, stats, everyone, (th, tl), (gh, gl), e_own, e_far, u, order)
        )
        pin = units[-1][1]
    far_mine = column(peers, pin)
    for step in range(2):
        units = fold([(k_, swap(s_, g[step])) for g, (k_, s_) in zip(COLORS, units)])
    far_other = swap(far_mine, CORE)
    triples = [(k_, swap(s_, g[2]), o_) for g, (k_, s_), o_ in zip(COLORS, units, shares)]
    weights, tick = final_weights(me, stats, everyone, e_own, (xh, xl), far_mine, far_other)
    mine, theirs = last_update(me, triples)
    return weights, place(me, tick, mine, swap(theirs, ZG))


def place_kernel(me_ref, pin_ref, mine_ref, other_ref, out_ref):
    z = me_ref[0] // 8
    width = mine_ref.shape[1]
    out_ref[:, pl.ds(pl.multiple_of(z * width, width), width)] = mine_ref[...]
    out_ref[:, pl.ds(pl.multiple_of((1 - z) * width, width), width)] = other_ref[...]


def place(me, pin, mine, other):
    rows, width = mine.shape
    return pl.pallas_call(
        place_kernel,
        in_specs=[SMALL, ANY, NEAR, NEAR],
        out_specs=NEAR,
        out_shape=jax.ShapeDtypeStruct((rows, 2 * width), F32),
        compiler_params=params(4),
        cost_estimate=cost(1, 16 * rows * width),
        name="place",
    )(me, pin, mine, other)


def solution(mesh):
    placed = (P("pts", None), P(None, "cen"))
    return jax.shard_map(
        local,
        mesh=mesh,
        in_specs=placed,
        out_specs=(P("pts", "cen"), P("pts", "cen")),
        check_vma=False,
    )
```

time: 556 us -> 182 us (0.33); the launches traced: 548 us -> 182 us
  blocking collectives: 234 us -> 30.7 us
  waiting for transfers between devices: 190 us -> 61 us
  matrix products: 60.7 us -> 0 us
  starting transfers between devices: 0.29 us -> 44.7 us
  Pallas kernels: 0 us -> 44.4 us
  local copies, waits for them, and re-layouts: 26.4 us -> 0.03 us
  other arithmetic: 22.2 us -> 0.08 us
  between operations: 14.3 us -> 0.85 us
    psum x4 -> x0, blocking collectives: 162 us -> none  [the longest x2 85.5 us: count_sum(): return lax.psum(jnp.sum(weights, axis=0), 'pts')]
    unnamed x5 -> x0, waiting for transfers between devices: 118 us -> none
    all_gather x1 -> x0, waiting for transfers between devices: 72.7 us -> none  [local(): piece = lax.all_gather(share, 'pts', axis=0, tiled=True)]
    pmax x2 -> x0, blocking collectives: 71.6 us -> none  [soft_weights(): top = lax.pmax(local_top, 'cen')]
    ppermute x0 -> x32, waiting for transfers between devices: none -> 61 us  [the longest x25 53.5 us: swap(): lax.ppermute(v, 'pts', [(i, i ^ g) for i in range(lax.axis_size('pts'))])]
    dot_general x4 -> x0, matrix products: 60.7 us -> none  [the longest x2 27.2 us: moment_share(): lax.dot_general(sample_vectors, weights, (((0,), (0,)), ((), ())), precis...]
    ppermute x0 -> x32, starting transfers between devices: none -> 44.7 us  [the longest x25 36.5 us: swap(): lax.ppermute(v, 'pts', [(i, i ^ g) for i in range(lax.axis_size('pts'))])]
    pallas_call x0 -> x26, Pallas kernels: none -> 44.4 us  [the longest x1 11 us: first_step(): pl.pallas_call(first_kernel, grid=(n // tile,), in_specs=[SMALL, SMALL, A...]
  transfers between devices with their start and end apart: 3 -> 32, of which waited for: 3 -> 22; matrix products, arithmetic and copies ran while one was open for 2% -> 0% of each run, Pallas kernels for 0% -> 20%
where the time goes in v2:
time: 182 us
  waiting for transfers between devices  61 us (34%)
  starting transfers between devices  44.7 us (25%)
  Pallas kernels  44.4 us (24%)
  blocking collectives  30.7 us (17%)
    ppermute x25, waiting for transfers between devices, swap(): lax.ppermute(v, 'pts', [(i, i ^ g) for i in range(lax.axis_size('pts'))])  53.5 us
    ppermute x25, starting transfers between devices, swap(): lax.ppermute(v, 'pts', [(i, i ^ g) for i in range(lax.axis_size('pts'))])  36.5 us
    all_to_all x1, blocking collectives, local(): lax.all_to_all(merge(joint, stats, swap(stats, ZG), cen), 'cen', 0, 0)  17.7 us
    all_to_all x1, blocking collectives, local(): everyone = lax.all_to_all(copies, 'cen', 0, 0)  13 us
    pallas_call x1, Pallas kernels, first_step(): pl.pallas_call(first_kernel, grid=(n // tile,), in_specs=[SMALL, SMALL, A...  11 us
    pallas_call x1, Pallas kernels, final_weights(): pl.pallas_call(weights_kernel, grid_spec=pltpu.PrefetchScalarGridSpec(num...  6.26 us
    pallas_call x2, Pallas kernels, next_moments(): pl.pallas_call(functools.partial(next_moment_kernel, order, color), in_sp...  5.89 us
    pallas_call x2, Pallas kernels, first_moments(): pl.pallas_call(functools.partial(first_moment_kernel, order, color), in_s...  5.64 us
  transfers between devices with their start and end apart: 32, of which 22 were waited for; matrix products, arithmetic and copies ran while one was open for 0% of the time, Pallas kernels for 20%

profile of v2, /device:TPU:8, one launch (start us, length us, event | category | flops | bytes accessed | tf_op | source)
XLA Modules:
  0.0 181.8 jit_solution(11387684005582116753)
XLA Ops:
  0.7 1.6 own_piece.1.pin_ref
  2.3 7.3 %collective-permute-start = (f32[768,128]{1,0:T(8,128)S(1)}, f32[768,128]{1,0:T(8,128)S(1)}, u32[]{:S(2)}, u32[]{:S(2)}) collective-permute-start(f32[768,128]{1,0:T(8,128)S(1)} %own_piece.1.pin_ref), channel_id=1, source_target_pairs={{0,128},{16,144},{32,160},{48,176},{64,192},{80,208},{96,224},{112... | collective-permute-start | bytes 1179656 | tf_op jit(solution)/shard_map/ppermute | solution.py:37
  9.6 11.0 %first_logits.1 = (f32[768,1024]{1,0:T(8,128)S(1)}, f32[2,768]{1,0:T(2,128)S(1)}, f32[16,2,768]{2,1,0:T(2,128)S(1)}, bf16[768,1024]{1,0:T(8,128)(2,1)}, bf16[768...) custom-call(s32[1]{0:T(128)} %bitcast.me_ref.at_ref, s32[4]{0:T(128)S(1)} %pad_add_fusion.at_ref, ...), custom_call_target="tpu_custom_call" | custom-call | flops 9663676416 | bytes 1363148 | tf_op jit(solution)/shard_map/first_logits/pallas_call | solution.py:106
  20.5 13.0 %all_to_all.10.all_ref = f32[16,2,768]{2,1,0:T(2,128)S(1)} all-to-all(f32[16,2,768]{2,1,0:T(2,128)S(1)} %get-tuple-element.60), channel_id=1, replica_groups=mesh['pts'=16,'cen'=16] {'cen'}, dimensions={0} | all-to-all | bytes 196608 | tf_op jit(solution)/shard_map/all_to_all | solution.py:701
  33.5 2.8 %first_moments.2 = (f32[520,512]{1,0:T(8,128)S(1)}, f32[520,512]{1,0:T(8,128)S(1)}) custom-call(s32[1]{0:T(128)} %bitcast.me_ref.at_ref, f32[768,128]{1,0:T(8,128)S(1)} %collective-permute-done.pin_ref.mine_ref, f32[2,768]{1,0:T(2,128)S(1)} %get-tuple-element.59.own_ref, f32[16,2,768]{2,1,0:T(2,128)S(1)} %all_to_all.10.all_ref, ...), custom_call_target="tpu_custom_call" | custom-call | flops 241591904 | bytes 681574 | tf_op jit(solution)/shard_map/first_moments/pallas_call | solution.py:394
  36.4 2.8 %first_moments.3 = (f32[520,512]{1,0:T(8,128)S(1)}, f32[520,512]{1,0:T(8,128)S(1)}) custom-call(s32[1]{0:T(128)} %bitcast.me_ref.at_ref, f32[520,512]{1,0:T(8,128)S(1)} %get-tuple-element.64.pin_ref, f32[2,768]{1,0:T(2,128)S(1)} %get-tuple-element.59.own_ref, f32[16,2,768]{2,1,0:T(2,128)S(1)} %all_to_all.10.all_ref, ...), custom_call_target="tpu_custom_call" | custom-call | flops 241591904 | bytes 681574 | tf_op jit(solution)/shard_map/first_moments/pallas_call | solution.py:394
  40.2 1.8 collective-permute-done.6.refs_3_
  42.0 1.5 collective-permute-done.5.refs_1_
  43.8 1.6 collective-permute-start.7
  45.3 2.1 %collective-permute-start.8 = (f32[264,512]{1,0:T(8,128)S(1)}, f32[264,512]{1,0:T(8,128)S(1)}, u32[]{:S(2)}, u32[]{:S(2)}) collective-permute-start(f32[264,512]{1,0:T(8,128)S(1)} %get-tuple-element.71), channel_id=1, source_target_pairs={{0,96},{16,112},{32,64},{48,80},{64,32},{80,48},{96,0},{112,16},{1... | collective-permute-start | bytes 1622024 | tf_op jit(solution)/shard_map/ppermute | solution.py:37
  47.4 1.0 old_block.1.pin_ref.refs_6_
  48.4 2.6 %collective-permute-done.1.other_ref = f32[768,128]{1,0:T(8,128)S(1)} collective-permute-done((f32[768,128]{1,0:T(8,128)S(1)}, f32[768,128]{1,0:T(8,128)S(1)}, u32[]{:S(2)}, u32[]{:S(2)}) %collective-permute-start.1) | collective-permute-done | bytes 393248 | tf_op jit(solution)/shard_map/ppermute | solution.py:707
  51.6 1.5 collective-permute-start.4
  53.7 2.7 %collective-permute-start.2 = (f32[768,256]{1,0:T(8,128)S(1)}, f32[768,256]{1,0:T(8,128)S(1)}, u32[]{:S(2)}, u32[]{:S(2)}) collective-permute-start(f32[768,256]{1,0:T(8,128)S(1)} %couple.1.refs_0_), channel_id=1, source_target_pairs={{0,8},{1,9},{2,10},{3,11},{4,12},{5,13},{6,14},{7,15},{8,0},{9,1},... | collective-permute-start | bytes 2359304 | tf_op jit(solution)/shard_map/ppermute | solution.py:694
  56.4 1.7 collective-permute-done.7.refs_2_
  58.2 2.4 %collective-permute-done.8.refs_4_ = f32[264,512]{1,0:T(8,128)S(1)} collective-permute-done((f32[264,512]{1,0:T(8,128)S(1)}, f32[264,512]{1,0:T(8,128)S(1)}, u32[]{:S(2)}, u32[]{:S(2)}) %collective-permute-start.8) | collective-permute-done | bytes 540704 | tf_op jit(solution)/shard_map/ppermute | solution.py:37
  60.7 2.2 %collective-permute-start.9 = (f32[136,512]{1,0:T(8,128)S(1)}, f32[136,512]{1,0:T(8,128)S(1)}, u32[]{:S(2)}, u32[]{:S(2)}) collective-permute-start(f32[136,512]{1,0:T(8,128)S(1)} %get-tuple-element.73), channel_id=1, source_target_pairs={{0,96},{16,112},{32,64},{48,80},{64,32},{80,48},{96,0},{112,16},{1... | collective-permute-start | bytes 835592 | tf_op jit(solution)/shard_map/ppermute | solution.py:37
  62.9 6.7 %collective-permute-done.9.refs_1_ = f32[136,512]{1,0:T(8,128)S(1)} collective-permute-done((f32[136,512]{1,0:T(8,128)S(1)}, f32[136,512]{1,0:T(8,128)S(1)}, u32[]{:S(2)}, u32[]{:S(2)}) %collective-permute-start.9) | collective-permute-done | bytes 278560 | tf_op jit(solution)/shard_map/ppermute | solution.py:37
  70.2 2.4 %collective-permute-start.11 = (f32[136,256]{1,0:T(8,128)S(1)}, f32[136,256]{1,0:T(8,128)S(1)}, u32[]{:S(2)}, u32[]{:S(2)}) collective-permute-start(f32[136,256]{1,0:T(8,128)S(1)} %get-tuple-element.77), channel_id=1, source_target_pairs={{0,128},{16,144},{32,160},{48,176},{64,192},{80,208},{96,224},{112... | collective-permute-start | bytes 417800 | tf_op jit(solution)/shard_map/ppermute | solution.py:37
  72.6 3.6 %collective-permute-start.12 = (f32[136,256]{1,0:T(8,128)S(1)}, f32[136,256]{1,0:T(8,128)S(1)}, u32[]{:S(2)}, u32[]{:S(2)}) collective-permute-start(f32[136,256]{1,0:T(8,128)S(1)} %get-tuple-element.79), channel_id=1, source_target_pairs={{0,128},{16,144},{32,160},{48,176},{64,192},{80,208},{96,224},{112... | collective-permute-start | bytes 417800 | tf_op jit(solution)/shard_map/ppermute | solution.py:37
  76.3 5.7 %collective-permute-done.11.refs_3_ = f32[136,256]{1,0:T(8,128)S(1)} collective-permute-done((f32[136,256]{1,0:T(8,128)S(1)}, f32[136,256]{1,0:T(8,128)S(1)}, u32[]{:S(2)}, u32[]{:S(2)}) %collective-permute-start.11) | collective-permute-done | bytes 139296 | tf_op jit(solution)/shard_map/ppermute | solution.py:37
  82.0 3.2 %collective-permute-done.12.refs_5_ = f32[136,256]{1,0:T(8,128)S(1)} collective-permute-done((f32[136,256]{1,0:T(8,128)S(1)}, f32[136,256]{1,0:T(8,128)S(1)}, u32[]{:S(2)}, u32[]{:S(2)}) %collective-permute-start.12) | collective-permute-done | bytes 139296 | tf_op jit(solution)/shard_map/ppermute | solution.py:37
  85.2 1.8 collective-permute-start.13
  87.4 4.7 %collective-permute-done.13.refs_2_ = f32[128,256]{1,0:T(8,128)S(1)} collective-permute-done((f32[128,256]{1,0:T(8,128)S(1)}, f32[128,256]{1,0:T(8,128)S(1)}, u32[]{:S(2)}, u32[]{:S(2)}) %collective-permute-start.13) | collective-permute-done | bytes 131104 | tf_op jit(solution)/shard_map/ppermute | solution.py:37
  92.1 1.0 collective-permute-done.14.refs_4_
  93.4 1.7 collective-permute-start.16
  95.1 4.5 %collective-permute-done.15.refs_1_ = f32[256,256]{1,0:T(8,128)S(1)} collective-permute-done((f32[256,256]{1,0:T(8,128)S(1)}, f32[256,256]{1,0:T(8,128)S(1)}, u32[]{:S(2)}, u32[]{:S(2)}) %collective-permute-start.15) | collective-permute-done | bytes 262176 | tf_op jit(solution)/shard_map/ppermute | solution.py:37
  99.6 1.4 collective-permute-done.16.refs_3_
  102.5 1.5 far_points.1
  103.9 5.5 %own_logits.1 = (f32[768,512]{1,0:T(8,128)S(1)}, f32[2,768]{1,0:T(2,128)S(1)}, bf16[1024,512]{1,0:T(8,128)(2,1)S(1)}, bf16[1024,512]{1,0:T(8,128)(2,1)S(1)}, f32[8,512]{1,0:T(8,128)S(1)}) custom-call(s32[1]{0:T(128)} %bitcast.me_ref.at_ref, f32[512,256]{1,0:T(8,128)S(1)} %get-tuple-element.84.refs_0_, f32[512,256]{1,0:T(8,128)S(1)} %collective-permute-done.17.refs_1_, ...), custom_call_target="tpu_custom_call" | custom-call | flops 241591904 | bytes 681574 | tf_op jit(solution)/shard_map/own_logits/pallas_call | solution.py:270
  109.4 3.8 %far_logits.1 = (f32[768,512]{1,0:T(8,128)S(1)}, f32[2,1536]{1,0:T(2,128)S(1)}) custom-call(s32[1]{0:T(128)} %bitcast.me_ref.at_ref, bf16[1024,512]{1,0:T(8,128)(2,1)S(1)} %get-tuple-element.88.ch, bf16[1024,512]{1,0:T(8,128)(2,1)S(1)} %get-tuple-element.89.cl, f32[8,512]{1,0:T(8,128)S(1)} %get-tuple-element.90.norm, ...), custom_call_target="tpu_custom_call" | custom-call | flops 241591904 | bytes 681574 | tf_op jit(solution)/shard_map/far_logits/pallas_call | solution.py:312
  113.3 5.2 %collective-permute-start.20 = (f32[2,1536]{1,0:T(2,128)S(1)}, f32[2,1536]{1,0:T(2,128)S(1)}, u32[]{:S(2)}, u32[]{:S(2)}) collective-permute-start(f32[2,1536]{1,0:T(2,128)S(1)} %get-tuple-element.94.mine_ref.own.own_ref), channel_id=1, source_target_pairs={{0,128},{16,144},{32,160},{48,176},{64,192},{80,208},{96,224},{112... | collective-permute-start | bytes 36872 | tf_op jit(solution)/shard_map/ppermute | solution.py:37
  118.5 2.5 %collective-permute-done.20.other_ref = f32[2,1536]{1,0:T(2,128)S(1)} collective-permute-done((f32[2,1536]{1,0:T(2,128)S(1)}, f32[2,1536]{1,0:T(2,128)S(1)}, u32[]{:S(2)}, u32[]{:S(2)}) %collective-permute-start.20) | collective-permute-done | bytes 12320 | tf_op jit(solution)/shard_map/ppermute | solution.py:37
  121.0 17.7 %all_to_all.11.pin_ref.everyone.all_ref = f32[16,2,1536]{2,1,0:T(2,128)S(1)} all-to-all(f32[16,2,1536]{2,1,0:T(2,128)S(1)} %merge.1), channel_id=1, replica_groups=mesh['pts'=16,'cen'=16] {'cen'}, dimensions={0} | all-to-all | bytes 393216 | tf_op jit(solution)/shard_map/all_to_all | solution.py:722
  138.6 1.5 collective-permute-start.23
  140.2 1.1 collective-permute-start.22
  141.8 2.9 %next_moments.2 = (f32[520,256]{1,0:T(8,128)S(1)}, f32[520,256]{1,0:T(8,128)S(1)}) custom-call(s32[1]{0:T(128)} %bitcast.me_ref.at_ref, f32[16,2,1536]{2,1,0:T(2,128)S(1)} %all_to_all.11.pin_ref.everyone.all_ref, f32[2,1536]{1,0:T(2,128)S(1)} %get-tuple-element.94.mine_ref.own.own_ref, f32[16,2,1536]{2,1,0:T(2,128)S(1)} %all_to_all.11.pin_ref.everyone.all_ref, ...), custom_call_target="tpu_custom_call" | custom-call | flops 241591904 | bytes 891289 | tf_op jit(solution)/shard_map/next_moments/pallas_call | solution.py:428
  144.7 3.0 %next_moments.3 = (f32[520,256]{1,0:T(8,128)S(1)}, f32[520,256]{1,0:T(8,128)S(1)}) custom-call(s32[1]{0:T(128)} %bitcast.me_ref.at_ref, f32[520,256]{1,0:T(8,128)S(1)} %get-tuple-element.100.pin_ref, f32[2,1536]{1,0:T(2,128)S(1)} %get-tuple-element.94.mine_ref.own.own_ref, f32[16,2,1536]{2,1,0:T(2,128)S(1)} %all_to_all.11.pin_ref.everyone.all_ref, ...), custom_call_target="tpu_custom_call" | custom-call | flops 241591904 | bytes 891289 | tf_op jit(solution)/shard_map/next_moments/pallas_call | solution.py:428
  149.1 1.0 collective-permute-done.22.refs_2_
  150.0 2.7 %collective-permute-done.21.refs_1_ = f32[128,512]{1,0:T(8,128)S(1)} collective-permute-done((f32[128,512]{1,0:T(8,128)S(1)}, f32[128,512]{1,0:T(8,128)S(1)}, u32[]{:S(2)}, u32[]{:S(2)}) %collective-permute-start.21) | collective-permute-done | bytes 262176 | tf_op jit(solution)/shard_map/ppermute | solution.py:727
  153.2 1.5 collective-permute-start.28
  154.7 7.4 %collective-permute-done.27.refs_1_ = f32[264,256]{1,0:T(8,128)S(1)} collective-permute-done((f32[264,256]{1,0:T(8,128)S(1)}, f32[264,256]{1,0:T(8,128)S(1)}, u32[]{:S(2)}, u32[]{:S(2)}) %collective-permute-start.27) | collective-permute-done | bytes 270368 | tf_op jit(solution)/shard_map/ppermute | solution.py:37
  162.0 1.3 collective-permute-done.28.refs_3_
  163.4 1.2 collective-permute-start.29
  164.6 5.4 %collective-permute-done.29.refs_1_ = f32[136,256]{1,0:T(8,128)S(1)} collective-permute-done((f32[136,256]{1,0:T(8,128)S(1)}, f32[136,256]{1,0:T(8,128)S(1)}, u32[]{:S(2)}, u32[]{:S(2)}) %collective-permute-start.29) | collective-permute-done | bytes 139296 | tf_op jit(solution)/shard_map/ppermute | solution.py:37
  170.1 3.0 %collective-permute-start.31 = (f32[64,512]{1,0:T(8,128)S(1)}, f32[64,512]{1,0:T(8,128)S(1)}, u32[]{:S(2)}, u32[]{:S(2)}) collective-permute-start(f32[64,512]{1,0:T(8,128)S(1)} %get-tuple-element.115), channel_id=1, source_target_pairs={{0,128},{16,144},{32,160},{48,176},{64,192},{80,208},{96,224},{112... | collective-permute-start | bytes 393224 | tf_op jit(solution)/shard_map/ppermute | solution.py:37
  173.1 6.3 %weights.1 = (f32[768,1024]{1,0:T(8,128)}, f32[8,128]{1,0:T(8,128)S(1)}) custom-call(s32[1]{0:T(128)} %bitcast.me_ref.at_ref, f32[2,1536]{1,0:T(2,128)S(1)} %get-tuple-element.94.mine_ref.own.own_ref, f32[16,2,1536]{2,1,0:T(2,128)S(1)} %all_to_all.11.pin_ref.everyone.all_ref, f32[768,512]{1,0:T(8,128)S(1)} %get-tuple-element.96.e0.e_ref, ...), custom_call_target="tpu_custom_call" | custom-call | flops 241591904 | bytes 996147 | tf_op jit(solution)/shard_map/weights/pallas_call | solution.py:654
  179.3 1.7 collective-permute-done.31.other_ref
  (46 shorter events, 8.7 us)
Async XLA Ops:
  2.3 31.2 %collective-permute-start = (f32[768,128]{1,0:T(8,128)S(1)}, f32[768,128]{1,0:T(8,128)S(1)}, u32[]{:S(2)}, u32[]{:S(2)}) collective-permute-start(f32[768,128]{1,0:T(8,128)S(1)} %own_piece.1.pin_ref), channel_id=1, source_target_pairs={{0,128},{16,144},{32,160},{48,176},{64,192},{80,208},{96,224},{112... | collective-permute-start | bytes 1179656 | tf_op jit(solution)/shard_map/ppermute | solution.py:37
  39.2 2.8 %collective-permute-start.6 = (f32[520,512]{1,0:T(8,128)S(1)}, f32[520,512]{1,0:T(8,128)S(1)}, u32[]{:S(2)}, u32[]{:S(2)}) collective-permute-start(f32[520,512]{1,0:T(8,128)S(1)} %get-tuple-element.65.pin_ref), channel_id=1, source_target_pairs={{0,16},{16,0},{32,48},{48,32},{64,80},{80,64},{96,112},{112,96},{1... | collective-permute-start | bytes 3194888 | tf_op jit(solution)/shard_map/ppermute | solution.py:37
  39.3 4.2 %collective-permute-start.5 = (f32[520,512]{1,0:T(8,128)S(1)}, f32[520,512]{1,0:T(8,128)S(1)}, u32[]{:S(2)}, u32[]{:S(2)}) collective-permute-start(f32[520,512]{1,0:T(8,128)S(1)} %get-tuple-element.64.pin_ref), channel_id=1, source_target_pairs={{0,16},{16,0},{32,48},{48,32},{64,80},{80,64},{96,112},{112,96},{1... | collective-permute-start | bytes 3194888 | tf_op jit(solution)/shard_map/ppermute | solution.py:37
  39.8 11.2 %collective-permute-start.1 = (f32[768,128]{1,0:T(8,128)S(1)}, f32[768,128]{1,0:T(8,128)S(1)}, u32[]{:S(2)}, u32[]{:S(2)}) collective-permute-start(f32[768,128]{1,0:T(8,128)S(1)} %relay.2), channel_id=1, source_target_pairs={{0,1},{1,0},{2,3},{3,2},{4,5},{5,4},{6,7},{7,6},{8,9},{9,8},{10,11... | collective-permute-start | bytes 1179656 | tf_op jit(solution)/shard_map/ppermute | solution.py:707
  43.8 14.4 %collective-permute-start.7 = (f32[264,512]{1,0:T(8,128)S(1)}, f32[264,512]{1,0:T(8,128)S(1)}, u32[]{:S(2)}, u32[]{:S(2)}) collective-permute-start(f32[264,512]{1,0:T(8,128)S(1)} %get-tuple-element.69), channel_id=1, source_target_pairs={{0,32},{16,48},{32,0},{48,16},{64,96},{80,112},{96,64},{112,80},{1... | collective-permute-start | bytes 1622024 | tf_op jit(solution)/shard_map/ppermute | solution.py:37
  45.3 15.2 %collective-permute-start.8 = (f32[264,512]{1,0:T(8,128)S(1)}, f32[264,512]{1,0:T(8,128)S(1)}, u32[]{:S(2)}, u32[]{:S(2)}) collective-permute-start(f32[264,512]{1,0:T(8,128)S(1)} %get-tuple-element.71), channel_id=1, source_target_pairs={{0,96},{16,112},{32,64},{48,80},{64,32},{80,48},{96,0},{112,16},{1... | collective-permute-start | bytes 1622024 | tf_op jit(solution)/shard_map/ppermute | solution.py:37
  51.6 24.6 %collective-permute-start.4 = (f32[768,256]{1,0:T(8,128)S(1)}, f32[768,256]{1,0:T(8,128)S(1)}, u32[]{:S(2)}, u32[]{:S(2)}) collective-permute-start(f32[768,256]{1,0:T(8,128)S(1)} %couple.1.refs_0_), channel_id=1, source_target_pairs={{0,12},{1,13},{2,14},{3,15},{4,0},{5,1},{6,2},{7,3},{8,4},{9,5},{1... | collective-permute-start | bytes 2359304 | tf_op jit(solution)/shard_map/ppermute | solution.py:694
  53.2 23.1 %collective-permute-start.3 = (f32[768,256]{1,0:T(8,128)S(1)}, f32[768,256]{1,0:T(8,128)S(1)}, u32[]{:S(2)}, u32[]{:S(2)}) collective-permute-start(f32[768,256]{1,0:T(8,128)S(1)} %couple.1.refs_0_), channel_id=1, source_target_pairs={{0,4},{1,5},{2,6},{3,7},{4,8},{5,9},{6,10},{7,11},{8,12},{9,13},{1... | collective-permute-start | bytes 2359304 | tf_op jit(solution)/shard_map/ppermute | solution.py:694
  53.7 33.7 %collective-permute-start.2 = (f32[768,256]{1,0:T(8,128)S(1)}, f32[768,256]{1,0:T(8,128)S(1)}, u32[]{:S(2)}, u32[]{:S(2)}) collective-permute-start(f32[768,256]{1,0:T(8,128)S(1)} %couple.1.refs_0_), channel_id=1, source_target_pairs={{0,8},{1,9},{2,10},{3,11},{4,12},{5,13},{6,14},{7,15},{8,0},{9,1},... | collective-permute-start | bytes 2359304 | tf_op jit(solution)/shard_map/ppermute | solution.py:694
  60.7 8.8 %collective-permute-start.9 = (f32[136,512]{1,0:T(8,128)S(1)}, f32[136,512]{1,0:T(8,128)S(1)}, u32[]{:S(2)}, u32[]{:S(2)}) collective-permute-start(f32[136,512]{1,0:T(8,128)S(1)} %get-tuple-element.73), channel_id=1, source_target_pairs={{0,96},{16,112},{32,64},{48,80},{64,32},{80,48},{96,0},{112,16},{1... | collective-permute-start | bytes 835592 | tf_op jit(solution)/shard_map/ppermute | solution.py:37
  62.9 7.3 %collective-permute-start.10 = (f32[136,512]{1,0:T(8,128)S(1)}, f32[136,512]{1,0:T(8,128)S(1)}, u32[]{:S(2)}, u32[]{:S(2)}) collective-permute-start(f32[136,512]{1,0:T(8,128)S(1)} %get-tuple-element.75), channel_id=1, source_target_pairs={{0,32},{16,48},{32,0},{48,16},{64,96},{80,112},{96,64},{112,80},{1... | collective-permute-start | bytes 835592 | tf_op jit(solution)/shard_map/ppermute | solution.py:37
  70.2 11.8 %collective-permute-start.11 = (f32[136,256]{1,0:T(8,128)S(1)}, f32[136,256]{1,0:T(8,128)S(1)}, u32[]{:S(2)}, u32[]{:S(2)}) collective-permute-start(f32[136,256]{1,0:T(8,128)S(1)} %get-tuple-element.77), channel_id=1, source_target_pairs={{0,128},{16,144},{32,160},{48,176},{64,192},{80,208},{96,224},{112... | collective-permute-start | bytes 417800 | tf_op jit(solution)/shard_map/ppermute | solution.py:37
  72.6 12.5 %collective-permute-start.12 = (f32[136,256]{1,0:T(8,128)S(1)}, f32[136,256]{1,0:T(8,128)S(1)}, u32[]{:S(2)}, u32[]{:S(2)}) collective-permute-start(f32[136,256]{1,0:T(8,128)S(1)} %get-tuple-element.79), channel_id=1, source_target_pairs={{0,128},{16,144},{32,160},{48,176},{64,192},{80,208},{96,224},{112... | collective-permute-start | bytes 417800 | tf_op jit(solution)/shard_map/ppermute | solution.py:37
  85.2 6.9 %collective-permute-start.13 = (f32[128,256]{1,0:T(8,128)S(1)}, f32[128,256]{1,0:T(8,128)S(1)}, u32[]{:S(2)}, u32[]{:S(2)}) collective-permute-start(f32[128,256]{1,0:T(8,128)S(1)} %get-tuple-element.80.refs_1_.refs_2_), channel_id=1, source_target_pairs={{0,96},{16,112},{32,64},{48,80},{64,32},{80,48},{96,0},{112,16},{1... | collective-permute-start | bytes 393224 | tf_op jit(solution)/shard_map/ppermute | solution.py:37
  87.0 6.1 %collective-permute-start.14 = (f32[128,256]{1,0:T(8,128)S(1)}, f32[128,256]{1,0:T(8,128)S(1)}, u32[]{:S(2)}, u32[]{:S(2)}) collective-permute-start(f32[128,256]{1,0:T(8,128)S(1)} %get-tuple-element.81.refs_3_.refs_5_), channel_id=1, source_target_pairs={{0,32},{16,48},{32,0},{48,16},{64,96},{80,112},{96,64},{112,80},{1... | collective-permute-start | bytes 393224 | tf_op jit(solution)/shard_map/ppermute | solution.py:37
  93.2 6.5 %collective-permute-start.15 = (f32[256,256]{1,0:T(8,128)S(1)}, f32[256,256]{1,0:T(8,128)S(1)}, u32[]{:S(2)}, u32[]{:S(2)}) collective-permute-start(f32[256,256]{1,0:T(8,128)S(1)} %get-tuple-element.82.refs_0_), channel_id=1, source_target_pairs={{0,32},{16,48},{32,0},{48,16},{64,96},{80,112},{96,64},{112,80},{1... | collective-permute-start | bytes 786440 | tf_op jit(solution)/shard_map/ppermute | solution.py:37
  93.4 7.6 %collective-permute-start.16 = (f32[256,256]{1,0:T(8,128)S(1)}, f32[256,256]{1,0:T(8,128)S(1)}, u32[]{:S(2)}, u32[]{:S(2)}) collective-permute-start(f32[256,256]{1,0:T(8,128)S(1)} %get-tuple-element.83.refs_2_), channel_id=1, source_target_pairs={{0,96},{16,112},{32,64},{48,80},{64,32},{80,48},{96,0},{112,16},{1... | collective-permute-start | bytes 786440 | tf_op jit(solution)/shard_map/ppermute | solution.py:37
  101.1 2.9 %collective-permute-start.17 = (f32[512,256]{1,0:T(8,128)S(1)}, f32[512,256]{1,0:T(8,128)S(1)}, u32[]{:S(2)}, u32[]{:S(2)}) collective-permute-start(f32[512,256]{1,0:T(8,128)S(1)} %get-tuple-element.84.refs_0_), channel_id=1, source_target_pairs={{0,16},{16,0},{32,48},{48,32},{64,80},{80,64},{96,112},{112,96},{1... | collective-permute-start | bytes 1572872 | tf_op jit(solution)/shard_map/ppermute | solution.py:37
  101.2 2.8 %collective-permute-start.18 = (f32[512,256]{1,0:T(8,128)S(1)}, f32[512,256]{1,0:T(8,128)S(1)}, u32[]{:S(2)}, u32[]{:S(2)}) collective-permute-start(f32[512,256]{1,0:T(8,128)S(1)} %get-tuple-element.85.refs_2_), channel_id=1, source_target_pairs={{0,16},{16,0},{32,48},{48,32},{64,80},{80,64},{96,112},{112,96},{1... | collective-permute-start | bytes 1572872 | tf_op jit(solution)/shard_map/ppermute | solution.py:37
  101.7 16.8 %collective-permute-start.19 = (f32[128,512]{1,0:T(8,128)S(1)}, f32[128,512]{1,0:T(8,128)S(1)}, u32[]{:S(2)}, u32[]{:S(2)}) collective-permute-start(f32[128,512]{1,0:T(8,128)S(1)} %get-tuple-element.95), channel_id=1, source_target_pairs={{0,128},{16,144},{32,160},{48,176},{64,192},{80,208},{96,224},{112... | collective-permute-start | bytes 786440 | tf_op jit(solution)/shard_map/ppermute | solution.py:37
  113.3 7.7 %collective-permute-start.20 = (f32[2,1536]{1,0:T(2,128)S(1)}, f32[2,1536]{1,0:T(2,128)S(1)}, u32[]{:S(2)}, u32[]{:S(2)}) collective-permute-start(f32[2,1536]{1,0:T(2,128)S(1)} %get-tuple-element.94.mine_ref.own.own_ref), channel_id=1, source_target_pairs={{0,128},{16,144},{32,160},{48,176},{64,192},{80,208},{96,224},{112... | collective-permute-start | bytes 36872 | tf_op jit(solution)/shard_map/ppermute | solution.py:37
  138.6 10.4 %collective-permute-start.23 = (f32[128,512]{1,0:T(8,128)S(1)}, f32[128,512]{1,0:T(8,128)S(1)}, u32[]{:S(2)}, u32[]{:S(2)}) collective-permute-start(f32[128,512]{1,0:T(8,128)S(1)} %relay.3.refs_0_), channel_id=1, source_target_pairs={{0,96},{16,112},{32,0},{48,16},{64,32},{80,48},{96,64},{112,80},{1... | collective-permute-start | bytes 786440 | tf_op jit(solution)/shard_map/ppermute | solution.py:727
  140.2 9.9 %collective-permute-start.22 = (f32[128,512]{1,0:T(8,128)S(1)}, f32[128,512]{1,0:T(8,128)S(1)}, u32[]{:S(2)}, u32[]{:S(2)}) collective-permute-start(f32[128,512]{1,0:T(8,128)S(1)} %relay.3.refs_0_), channel_id=1, source_target_pairs={{0,64},{16,80},{32,96},{48,112},{64,0},{80,16},{96,32},{112,48},{1... | collective-permute-start | bytes 786440 | tf_op jit(solution)/shard_map/ppermute | solution.py:727
  141.3 11.4 %collective-permute-start.21 = (f32[128,512]{1,0:T(8,128)S(1)}, f32[128,512]{1,0:T(8,128)S(1)}, u32[]{:S(2)}, u32[]{:S(2)}) collective-permute-start(f32[128,512]{1,0:T(8,128)S(1)} %relay.3.refs_0_), channel_id=1, source_target_pairs={{0,32},{16,48},{32,64},{48,80},{64,96},{80,112},{96,0},{112,16},{1... | collective-permute-start | bytes 786440 | tf_op jit(solution)/shard_map/ppermute | solution.py:727
  147.7 5.3 %collective-permute-start.26 = (f32[520,256]{1,0:T(8,128)S(1)}, f32[520,256]{1,0:T(8,128)S(1)}, u32[]{:S(2)}, u32[]{:S(2)}) collective-permute-start(f32[520,256]{1,0:T(8,128)S(1)} %get-tuple-element.101.pin_ref), channel_id=1, source_target_pairs={{0,16},{16,0},{32,48},{48,32},{64,80},{80,64},{96,112},{112,96},{1... | collective-permute-start | bytes 1597448 | tf_op jit(solution)/shard_map/ppermute | solution.py:37
  147.8 5.2 %collective-permute-start.25 = (f32[520,256]{1,0:T(8,128)S(1)}, f32[520,256]{1,0:T(8,128)S(1)}, u32[]{:S(2)}, u32[]{:S(2)}) collective-permute-start(f32[520,256]{1,0:T(8,128)S(1)} %get-tuple-element.100.pin_ref), channel_id=1, source_target_pairs={{0,16},{16,0},{32,48},{48,32},{64,80},{80,64},{96,112},{112,96},{1... | collective-permute-start | bytes 1597448 | tf_op jit(solution)/shard_map/ppermute | solution.py:37
  152.8 20.3 %collective-permute-start.24 = (f32[512,512]{1,0:T(8,128)S(1)}, f32[512,512]{1,0:T(8,128)S(1)}, u32[]{:S(2)}, u32[]{:S(2)}) collective-permute-start(f32[512,512]{1,0:T(8,128)S(1)} %column.1.mine_ref), channel_id=1, source_target_pairs={{0,16},{16,0},{32,48},{48,32},{64,80},{80,64},{96,112},{112,96},{1... | collective-permute-start | bytes 3145736 | tf_op jit(solution)/shard_map/ppermute | solution.py:37
  153.1 9.0 %collective-permute-start.27 = (f32[264,256]{1,0:T(8,128)S(1)}, f32[264,256]{1,0:T(8,128)S(1)}, u32[]{:S(2)}, u32[]{:S(2)}) collective-permute-start(f32[264,256]{1,0:T(8,128)S(1)} %get-tuple-element.107), channel_id=1, source_target_pairs={{0,32},{16,48},{32,0},{48,16},{64,96},{80,112},{96,64},{112,80},{1... | collective-permute-start | bytes 811016 | tf_op jit(solution)/shard_map/ppermute | solution.py:37
  153.2 10.2 %collective-permute-start.28 = (f32[264,256]{1,0:T(8,128)S(1)}, f32[264,256]{1,0:T(8,128)S(1)}, u32[]{:S(2)}, u32[]{:S(2)}) collective-permute-start(f32[264,256]{1,0:T(8,128)S(1)} %get-tuple-element.109), channel_id=1, source_target_pairs={{0,96},{16,112},{32,64},{48,80},{64,32},{80,48},{96,0},{112,16},{1... | collective-permute-start | bytes 811016 | tf_op jit(solution)/shard_map/ppermute | solution.py:37
  163.4 6.6 %collective-permute-start.29 = (f32[136,256]{1,0:T(8,128)S(1)}, f32[136,256]{1,0:T(8,128)S(1)}, u32[]{:S(2)}, u32[]{:S(2)}) collective-permute-start(f32[136,256]{1,0:T(8,128)S(1)} %get-tuple-element.111), channel_id=1, source_target_pairs={{0,96},{16,112},{32,64},{48,80},{64,32},{80,48},{96,0},{112,16},{1... | collective-permute-start | bytes 417800 | tf_op jit(solution)/shard_map/ppermute | solution.py:37
  164.6 5.4 %collective-permute-start.30 = (f32[136,256]{1,0:T(8,128)S(1)}, f32[136,256]{1,0:T(8,128)S(1)}, u32[]{:S(2)}, u32[]{:S(2)}) collective-permute-start(f32[136,256]{1,0:T(8,128)S(1)} %get-tuple-element.113), channel_id=1, source_target_pairs={{0,32},{16,48},{32,0},{48,16},{64,96},{80,112},{96,64},{112,80},{1... | collective-permute-start | bytes 417800 | tf_op jit(solution)/shard_map/ppermute | solution.py:37
  170.1 11.0 %collective-permute-start.31 = (f32[64,512]{1,0:T(8,128)S(1)}, f32[64,512]{1,0:T(8,128)S(1)}, u32[]{:S(2)}, u32[]{:S(2)}) collective-permute-start(f32[64,512]{1,0:T(8,128)S(1)} %get-tuple-element.115), channel_id=1, source_target_pairs={{0,128},{16,144},{32,160},{48,176},{64,192},{80,208},{96,224},{112... | collective-permute-start | bytes 393224 | tf_op jit(solution)/shard_map/ppermute | solution.py:37
